TPU v7x, 512 devices: a whole 4x8x8 slice. The times are simulated.
512 devices in a mesh: gene: 16 (over y, z_lo), prot: 32 (over x, z_hi, core).
Axes of the slice: x: 4, y: 8, z: 8 (z_hi: 4, z_lo: 2; z = z_hi * 2 + z_lo), core: 2. Of those that a mesh axis runs over, the one named last changes fastest.
Arguments:
- density: float32 [256, 192, 16, 128], P('gene', 'prot'), may hold values from 0 to 2
- levels: float32 [8], replicated, may hold values from 0.1 to 0.9
- rate_index: int32 [256, 3], P('gene'), may hold values from 0 to 7
- on_rate: float32 [8], replicated, may hold values from 0.2 to 3
- off_rate: float32 [8], replicated, may hold values from 0.2 to 3
- gene_order: int32 [4], replicated, may hold values from 0 to 3, each once
Outputs:
- evolved: float32 [256, 192, 16, 128], P('gene', 'prot')
Inputs may be any that keep to these rules, and one draw needn't show every extreme that they name: `gene_order`: a permutation of 0 to 3.
All inputs are finite; a program needn't handle non-finite values.
Results may differ from a plain program's by a relative error of at most 0.00002.
Values sent between devices are 32-bit elements; how exact they have to be, the bound alone decides.
No kernel may reach another device: no remote copies, remote signals or barrier semaphores. Data moves between devices by JAX's collectives and lax.ppermute only.
A program may use at most 64 MiB of HBM per device.

v0:
```python
from functools import partial

import jax
import jax.numpy as jnp
from jax import lax
from jax.sharding import PartitionSpec as P

STATE_BITS = 8
BLOCKS = 4
SUBSTEPS = 6


DIFF = 1.0
TIME_STEP = 0.15


def partner(value, axis, apart):
    mask = 2**apart
    pairs = [(source, source ^ mask) for source in range(lax.axis_size(axis))]
    return lax.ppermute(value, axis, pairs)


def extended(cells, sides, width):
    for axis, dim in sides:
        count = lax.axis_size(axis)
        ends = count - 1
        head = lax.slice_in_dim(cells, 0, width, axis=dim)
        tail = lax.slice_in_dim(cells, cells.shape[dim] - width, cells.shape[dim], axis=dim)
        cells = jnp.concatenate(
            [
                lax.ppermute(tail, axis, [(i, (i + 1) % count) for i in range(ends)]),
                cells,
                lax.ppermute(head, axis, [((i + 1) % count, i) for i in range(ends)]),
            ],
            axis=dim,
        )
    return cells


def along(field, drift, axis):
    pads = [(0, 0)] * 4
    pads[axis] = (1, 1)
    padded = jnp.pad(field, pads)
    dpad = jnp.pad(drift, pads)
    size = field.shape[axis]
    upper = lax.slice_in_dim(padded, 2, size + 2, axis=axis)
    lower = lax.slice_in_dim(padded, 0, size, axis=axis)
    d_up = lax.slice_in_dim(dpad, 2, size + 2, axis=axis)
    d_low = lax.slice_in_dim(dpad, 0, size, axis=axis)
    return DIFF * (upper - 2.0 * field + lower) - 0.5 * (d_up * upper - d_low * lower)


def substep(field, drift_x, drift_y, drift_z):
    change = along(field, drift_x, 1) + along(field, drift_y, 2) + along(field, drift_z, 3)
    return field + TIME_STEP * change


def partner_of(field, bit, local_bits):
    if bit < local_bits:
        count = field.shape[0]
        grouped = field.reshape((count >> bit + 1, 2, 1 << bit) + field.shape[1:])
        return grouped[:, ::-1].reshape(field.shape)
    return partner(field, "gene", bit - local_bits)


def local(density, levels, rate_index, on_rate, off_rate, gene_order):
    count, width_x, size_y, size_z = density.shape
    local_bits = count.bit_length() - 1
    total_x = width_x * lax.axis_size("prot")
    first_x = lax.axis_index("prot") * width_x
    state_ids = lax.axis_index("gene") * count + jnp.arange(count, dtype=jnp.int32)
    onehot = rate_index[:, :, None] == jnp.arange(levels.shape[0], dtype=jnp.int32)[None, None, :]
    level_of = jnp.sum(jnp.where(onehot, levels[None, None, :], 0.0), axis=-1)
    coord_y = (jnp.arange(size_y, dtype=jnp.float32) + 0.5) / size_y
    coord_z = (jnp.arange(size_z, dtype=jnp.float32) + 0.5) / size_z
    drift_y = (level_of[:, 1, None] - coord_y[None, :])[:, None, :, None]
    drift_z = (level_of[:, 2, None] - coord_z[None, :])[:, None, None, :]
    own_x = (first_x + jnp.arange(width_x, dtype=jnp.int32)).astype(jnp.float32)
    own_x = (own_x + 0.5) / total_x
    hill = 0.1 + own_x**2 / (0.09 + own_x**2)
    branches = [
        partial(partner_of, bit=STATE_BITS - 1 - k, local_bits=local_bits) for k in range(BLOCKS)
    ]
    field = density
    for block in range(BLOCKS):
        cells = first_x - SUBSTEPS + jnp.arange(width_x + 2 * SUBSTEPS, dtype=jnp.int32)
        inside = ((cells >= 0) & (cells < total_x)).astype(jnp.float32)[None, :, None, None]
        coord = (cells.astype(jnp.float32) + 0.5) / total_x
        drift_x, inside = ((level_of[:, 0, None] - coord[None, :])[:, :, None, None], inside)
        wide = extended(field, (("prot", 1),), SUBSTEPS)
        for step in range(SUBSTEPS):
            wide = substep(wide, drift_x, drift_y, drift_z) * inside
        field = wide[:, SUBSTEPS : SUBSTEPS + width_x]
        bit = STATE_BITS - 1 - gene_order[block]
        mate = lax.switch(gene_order[block], branches, field)
        high = (jnp.bitwise_and(jnp.right_shift(state_ids, bit), 1) == 1)[:, None, None, None]
        act = (on_rate[bit] * hill)[None, :, None, None]
        rate = act + off_rate[bit]
        share = act / rate
        decay = jnp.exp(-rate)
        low_part = jnp.where(high, mate, field)
        high_part = jnp.where(high, field, mate)
        total = low_part + high_part
        new_high = share * total + (high_part - share * total) * decay
        field = jnp.where(high, new_high, total - new_high)
    return field


def solution(mesh):
    in_specs = (P("gene", "prot", None, None), P(), P("gene", None), P(), P(), P())
    out_specs = P("gene", "prot", None, None)
    return jax.shard_map(local, mesh=mesh, in_specs=in_specs, out_specs=out_specs, check_vma=False)
```

profile of v0, /device:TPU:4, one launch (start us, length us, event | category | flops | bytes accessed | tf_op | source)
XLA Modules:
  0.0 346.8 jit_solution(12533535129919444825)
XLA Ops:
  1.9 10.4 %collective-permute-start.17 = (f32[16,6,16,128]{3,2,1,0:T(8,128)}, f32[16,6,16,128]{3,2,1,0:T(8,128)S(1)}, u32[]{:S(2)}, u32[]{:S(2)}) collective-permute-start(f32[16,6,16,128]{3,2,1,0:T(8,128)} %param.22), channel_id=1, source_target_pairs={{1,0},{2,1},{3,2},{4,3},{5,4},{6,5},{7,6},{8,7},{9,8},{10,9},{11,1... | collective-permute-start | bytes 2359304 | tf_op jit(solution)/shard_map/ppermute | solution.py:33
  26.0 4.5 %collective-permute-done.17 = f32[16,6,16,128]{3,2,1,0:T(8,128)S(1)} collective-permute-done((f32[16,6,16,128]{3,2,1,0:T(8,128)}, f32[16,6,16,128]{3,2,1,0:T(8,128)S(1)}, u32[]{:S(2)}, u32[]{:S(2)}) %collective-permute-start.17) | collective-permute-done | bytes 786464 | tf_op jit(solution)/shard_map/ppermute | solution.py:33
  30.6 3.6 %add_multiply_fusion.19 = f32[16,18,16,128]{3,2,1,0:T(8,128)S(1)} fusion(f32[16,18,16,128]{3,2,1,0:T(8,128)S(1)} %constant_dynamic-update-slice_fusion, f32[18]{0:T(128)S(1)} %and_convert_fusion, f32[16,128]{1,0:T(8,128)S(1)} %get-tuple-element.74, f32[16,128]{1,0:T(8,128)S(1)} %get-tuple-element.73, f32[16,16]{1,0:T(8,128)S(1)} %get-tuple-element.72, ...), kind=kLoop, calls=%fused_computation.243 | loop fusion | flops 15925248 | bytes 4739400 | tf_op jit(solution)/shard_map/mul | solution.py:92
  34.2 3.6 %add_multiply_fusion.18 = f32[16,18,16,128]{3,2,1,0:T(8,128)S(1)} fusion(f32[16,18,16,128]{3,2,1,0:T(8,128)S(1)} %add_multiply_fusion.19, f32[18]{0:T(128)S(1)} %and_convert_fusion, f32[16,128]{1,0:T(8,128)S(1)} %get-tuple-element.74, f32[16,128]{1,0:T(8,128)S(1)} %get-tuple-element.73, f32[16,16]{1,0:T(8,128)S(1)} %get-tuple-element.72, ...), kind=kLoop, calls=%fused_computation.239 | loop fusion | flops 15925248 | bytes 4739400 | tf_op jit(solution)/shard_map/mul | solution.py:92
  37.8 3.6 %add_multiply_fusion.17 = f32[16,18,16,128]{3,2,1,0:T(8,128)S(1)} fusion(f32[16,18,16,128]{3,2,1,0:T(8,128)S(1)} %add_multiply_fusion.18, f32[18]{0:T(128)S(1)} %and_convert_fusion, f32[16,128]{1,0:T(8,128)S(1)} %get-tuple-element.74, f32[16,128]{1,0:T(8,128)S(1)} %get-tuple-element.73, f32[16,16]{1,0:T(8,128)S(1)} %get-tuple-element.72, ...), kind=kLoop, calls=%fused_computation.235 | loop fusion | flops 15925248 | bytes 4739400 | tf_op jit(solution)/shard_map/mul | solution.py:92
  41.3 3.6 %add_multiply_fusion.16 = f32[16,18,16,128]{3,2,1,0:T(8,128)S(1)} fusion(f32[16,18,16,128]{3,2,1,0:T(8,128)S(1)} %add_multiply_fusion.17, f32[18]{0:T(128)S(1)} %and_convert_fusion, f32[16,128]{1,0:T(8,128)S(1)} %get-tuple-element.74, f32[16,128]{1,0:T(8,128)S(1)} %get-tuple-element.73, f32[16,16]{1,0:T(8,128)S(1)} %get-tuple-element.72, ...), kind=kLoop, calls=%fused_computation.231 | loop fusion | flops 15925248 | bytes 4739400 | tf_op jit(solution)/shard_map/mul | solution.py:92
  44.9 3.6 %add_multiply_fusion.15 = f32[16,18,16,128]{3,2,1,0:T(8,128)S(1)} fusion(f32[16,18,16,128]{3,2,1,0:T(8,128)S(1)} %add_multiply_fusion.16, f32[18]{0:T(128)S(1)} %and_convert_fusion, f32[16,128]{1,0:T(8,128)S(1)} %get-tuple-element.74, f32[16,128]{1,0:T(8,128)S(1)} %get-tuple-element.73, f32[16,16]{1,0:T(8,128)S(1)} %get-tuple-element.72, ...), kind=kLoop, calls=%fused_computation.227 | loop fusion | flops 15925248 | bytes 4739400 | tf_op jit(solution)/shard_map/mul | solution.py:92
  48.5 7.6 %subtract_add_fusion.7 = (f32[16,18,16,128]{3,2,1,0:T(8,128)}, f32[16,18,16,128]{3,2,1,0:T(8,128)}, f32[16,18,16,128]{3,2,1,0:T(8,128)}, f32[16,18,16,128]{3,2,1...) fusion(f32[16,18,16,128]{3,2,1,0:T(8,128)S(1)} %add_multiply_fusion.15, ...), kind=kLoop, calls=%fused_computation.226 | loop fusion | flops 10027008 | bytes 18895104 | tf_op jit(solution)/shard_map/add | solution.py:50
  59.4 37.9 %conditional.4 = (f32[16,6,16,128]{3,2,1,0:T(8,128)}) conditional(s32[]{:T(128)} %bitcast.19, f32[16,6,16,128]{3,2,1,0:T(8,128)S(1)} %fusion.55, f32[16,6,16,128]{3,2,1,0:T(8,128)S(1)} %fusion.55, f32[16,6,16,128]{3,2,1,0:T(8,128)S(1)} %fusion.55, f32[16,6,16,128]{3,2,1,0:T(8,128)S(1)} %fusion.55), branch_computations={%region_1.2_spmd, %region_2.3_spmd, %region_3.4_spmd, %region_4.5_... | conditional | bytes 3145776 | solution.py:95
  59.4 4.5 %collective-permute-start.1 = (f32[16,6,16,128]{3,2,1,0:T(8,128)S(1)}, f32[16,6,16,128]{3,2,1,0:T(8,128)}, u32[]{:S(2)}, u32[]{:S(2)}) collective-permute-start(f32[16,6,16,128]{3,2,1,0:T(8,128)S(1)} %param.1), channel_id=1, source_target_pairs={{0,128},{32,160},{64,192},{96,224},{128,0},{160,32},{192,64},{224,... | collective-permute-start | bytes 2359304 | tf_op jit(solution)/shard_map/cond/branch_1_fun/ppermute | solution.py:20
  63.9 33.3 %collective-permute-done.1 = f32[16,6,16,128]{3,2,1,0:T(8,128)} collective-permute-done((f32[16,6,16,128]{3,2,1,0:T(8,128)S(1)}, f32[16,6,16,128]{3,2,1,0:T(8,128)}, u32[]{:S(2)}, u32[]{:S(2)}) %collective-permute-start.1) | collective-permute-done | bytes 786464 | tf_op jit(solution)/shard_map/cond/branch_1_fun/ppermute | solution.py:20
  100.6 7.1 %collective-permute-start.19 = (f32[16,6,16,128]{3,2,1,0:T(8,128)S(1)}, f32[16,6,16,128]{3,2,1,0:T(8,128)S(1)}, u32[]{:S(2)}, u32[]{:S(2)}) collective-permute-start(f32[16,6,16,128]{3,2,1,0:T(8,128)S(1)} %subtract_select_fusion.3), channel_id=1, source_target_pairs={{1,0},{2,1},{3,2},{4,3},{5,4},{6,5},{7,6},{8,7},{9,8},{10,9},{11,1... | collective-permute-start | bytes 2359304 | tf_op jit(solution)/shard_map/ppermute | solution.py:33
  110.8 13.0 %collective-permute-done.18 = f32[16,6,16,128]{3,2,1,0:T(8,128)S(1)} collective-permute-done((f32[16,6,16,128]{3,2,1,0:T(8,128)S(1)}, f32[16,6,16,128]{3,2,1,0:T(8,128)S(1)}, u32[]{:S(2)}, u32[]{:S(2)}) %collective-permute-start.18) | collective-permute-done | bytes 786464 | tf_op jit(solution)/shard_map/ppermute | solution.py:31
  125.3 3.6 %add_multiply_fusion.14 = f32[16,18,16,128]{3,2,1,0:T(8,128)S(1)} fusion(f32[16,18,16,128]{3,2,1,0:T(8,128)S(1)} %pad_maximum_fusion, f32[18]{0:T(128)S(1)} %and_convert_fusion, f32[16,128]{1,0:T(8,128)S(1)} %get-tuple-element.74, f32[16,128]{1,0:T(8,128)S(1)} %get-tuple-element.73, f32[16,16]{1,0:T(8,128)S(1)} %get-tuple-element.72, ...), kind=kLoop, calls=%fused_computation.218 | loop fusion | flops 15925248 | bytes 4739400 | tf_op jit(solution)/shard_map/mul | solution.py:92
  128.9 3.6 %add_multiply_fusion.13 = f32[16,18,16,128]{3,2,1,0:T(8,128)S(1)} fusion(f32[16,18,16,128]{3,2,1,0:T(8,128)S(1)} %add_multiply_fusion.14, f32[18]{0:T(128)S(1)} %and_convert_fusion, f32[16,128]{1,0:T(8,128)S(1)} %get-tuple-element.74, f32[16,128]{1,0:T(8,128)S(1)} %get-tuple-element.73, f32[16,16]{1,0:T(8,128)S(1)} %get-tuple-element.72, ...), kind=kLoop, calls=%fused_computation.214 | loop fusion | flops 15925248 | bytes 4739400 | tf_op jit(solution)/shard_map/mul | solution.py:92
  132.4 3.6 %add_multiply_fusion.12 = f32[16,18,16,128]{3,2,1,0:T(8,128)S(1)} fusion(f32[16,18,16,128]{3,2,1,0:T(8,128)S(1)} %add_multiply_fusion.13, f32[18]{0:T(128)S(1)} %and_convert_fusion, f32[16,128]{1,0:T(8,128)S(1)} %get-tuple-element.74, f32[16,128]{1,0:T(8,128)S(1)} %get-tuple-element.73, f32[16,16]{1,0:T(8,128)S(1)} %get-tuple-element.72, ...), kind=kLoop, calls=%fused_computation.210 | loop fusion | flops 15925248 | bytes 4739400 | tf_op jit(solution)/shard_map/mul | solution.py:92
  136.0 3.6 %add_multiply_fusion.11 = f32[16,18,16,128]{3,2,1,0:T(8,128)S(1)} fusion(f32[16,18,16,128]{3,2,1,0:T(8,128)S(1)} %add_multiply_fusion.12, f32[18]{0:T(128)S(1)} %and_convert_fusion, f32[16,128]{1,0:T(8,128)S(1)} %get-tuple-element.74, f32[16,128]{1,0:T(8,128)S(1)} %get-tuple-element.73, f32[16,16]{1,0:T(8,128)S(1)} %get-tuple-element.72, ...), kind=kLoop, calls=%fused_computation.206 | loop fusion | flops 15925248 | bytes 4739400 | tf_op jit(solution)/shard_map/mul | solution.py:92
  143.2 7.6 %subtract_add_fusion.5 = (f32[16,18,16,128]{3,2,1,0:T(8,128)}, f32[16,18,16,128]{3,2,1,0:T(8,128)}, f32[16,18,16,128]{3,2,1,0:T(8,128)}, f32[16,18,16,128]{3,2,1...) fusion(f32[16,18,16,128]{3,2,1,0:T(8,128)S(1)} %add_multiply_fusion.10, ...), kind=kLoop, calls=%fused_computation.201 | loop fusion | flops 10027008 | bytes 18895104 | tf_op jit(solution)/shard_map/add | solution.py:50
  154.0 41.7 %conditional.5 = (f32[16,6,16,128]{3,2,1,0:T(8,128)}) conditional(s32[]{:T(128)} %bitcast.14, f32[16,6,16,128]{3,2,1,0:T(8,128)S(1)} %fusion.50, f32[16,6,16,128]{3,2,1,0:T(8,128)S(1)} %fusion.50, f32[16,6,16,128]{3,2,1,0:T(8,128)S(1)} %fusion.50, f32[16,6,16,128]{3,2,1,0:T(8,128)S(1)} %fusion.50), branch_computations={%region_5.6_spmd, %region_6.7_spmd, %region_7.8_spmd, %region_8.9_... | conditional | bytes 3145776 | solution.py:95
  154.0 7.8 %collective-permute-start.4 = (f32[16,6,16,128]{3,2,1,0:T(8,128)S(1)}, f32[16,6,16,128]{3,2,1,0:T(8,128)}, u32[]{:S(2)}, u32[]{:S(2)}) collective-permute-start(f32[16,6,16,128]{3,2,1,0:T(8,128)S(1)} %param.4), channel_id=1, source_target_pairs={{0,256},{32,288},{64,320},{96,352},{128,384},{160,416},{192,448},{... | collective-permute-start | bytes 2359304 | tf_op jit(solution)/shard_map/cond/branch_0_fun/ppermute | solution.py:20
  161.8 33.9 %collective-permute-done.4 = f32[16,6,16,128]{3,2,1,0:T(8,128)} collective-permute-done((f32[16,6,16,128]{3,2,1,0:T(8,128)S(1)}, f32[16,6,16,128]{3,2,1,0:T(8,128)}, u32[]{:S(2)}, u32[]{:S(2)}) %collective-permute-start.4) | collective-permute-done | bytes 786464 | tf_op jit(solution)/shard_map/cond/branch_0_fun/ppermute | solution.py:20
  199.1 6.9 %collective-permute-start.21 = (f32[16,6,16,128]{3,2,1,0:T(8,128)S(1)}, f32[16,6,16,128]{3,2,1,0:T(8,128)S(1)}, u32[]{:S(2)}, u32[]{:S(2)}) collective-permute-start(f32[16,6,16,128]{3,2,1,0:T(8,128)S(1)} %subtract_select_fusion.2), channel_id=1, source_target_pairs={{1,0},{2,1},{3,2},{4,3},{5,4},{6,5},{7,6},{8,7},{9,8},{10,9},{11,1... | collective-permute-start | bytes 2359304 | tf_op jit(solution)/shard_map/ppermute | solution.py:33
  209.1 12.8 %collective-permute-done.20 = f32[16,6,16,128]{3,2,1,0:T(8,128)S(1)} collective-permute-done((f32[16,6,16,128]{3,2,1,0:T(8,128)S(1)}, f32[16,6,16,128]{3,2,1,0:T(8,128)S(1)}, u32[]{:S(2)}, u32[]{:S(2)}) %collective-permute-start.20) | collective-permute-done | bytes 786464 | tf_op jit(solution)/shard_map/ppermute | solution.py:31
  240.0 7.6 %subtract_add_fusion.3 = (f32[16,18,16,128]{3,2,1,0:T(8,128)}, f32[16,18,16,128]{3,2,1,0:T(8,128)}, f32[16,18,16,128]{3,2,1,0:T(8,128)}, f32[16,18,16,128]{3,2,1...) fusion(f32[16,18,16,128]{3,2,1,0:T(8,128)S(1)} %add_multiply_fusion.5, ...), kind=kLoop, calls=%fused_computation.176 | loop fusion | flops 10027008 | bytes 18895104 | tf_op jit(solution)/shard_map/add | solution.py:50
  250.8 17.9 %conditional.6 = (f32[16,6,16,128]{3,2,1,0:T(8,128)}) conditional(s32[]{:T(128)} %bitcast.9, f32[16,6,16,128]{3,2,1,0:T(8,128)S(1)} %fusion.45, f32[16,6,16,128]{3,2,1,0:T(8,128)S(1)} %fusion.45, f32[16,6,16,128]{3,2,1,0:T(8,128)S(1)} %fusion.45, f32[16,6,16,128]{3,2,1,0:T(8,128)S(1)} %fusion.45), branch_computations={%region_9.10_spmd, %region_10.11_spmd, %region_11.12_spmd, %region... | conditional | bytes 3145776 | solution.py:95
  252.8 15.9 %collective-permute-done.10 = f32[16,6,16,128]{3,2,1,0:T(8,128)} collective-permute-done((f32[16,6,16,128]{3,2,1,0:T(8,128)S(1)}, f32[16,6,16,128]{3,2,1,0:T(8,128)}, u32[]{:S(2)}, u32[]{:S(2)}) %collective-permute-start.10) | collective-permute-done | bytes 786464 | tf_op jit(solution)/shard_map/cond/branch_2_fun/ppermute | solution.py:20
  272.1 6.9 %collective-permute-start.23 = (f32[16,6,16,128]{3,2,1,0:T(8,128)S(1)}, f32[16,6,16,128]{3,2,1,0:T(8,128)S(1)}, u32[]{:S(2)}, u32[]{:S(2)}) collective-permute-start(f32[16,6,16,128]{3,2,1,0:T(8,128)S(1)} %subtract_select_fusion.1), channel_id=1, source_target_pairs={{1,0},{2,1},{3,2},{4,3},{5,4},{6,5},{7,6},{8,7},{9,8},{10,9},{11,1... | collective-permute-start | bytes 2359304 | tf_op jit(solution)/shard_map/ppermute | solution.py:33
  282.3 12.6 %collective-permute-done.22 = f32[16,6,16,128]{3,2,1,0:T(8,128)S(1)} collective-permute-done((f32[16,6,16,128]{3,2,1,0:T(8,128)S(1)}, f32[16,6,16,128]{3,2,1,0:T(8,128)S(1)}, u32[]{:S(2)}, u32[]{:S(2)}) %collective-permute-start.22) | collective-permute-done | bytes 786464 | tf_op jit(solution)/shard_map/ppermute | solution.py:31
  304.0 3.6 %add_multiply_fusion.2 = f32[16,18,16,128]{3,2,1,0:T(8,128)S(1)} fusion(f32[16,18,16,128]{3,2,1,0:T(8,128)S(1)} %add_multiply_fusion.3, f32[18]{0:T(128)S(1)} %and_convert_fusion, f32[16,128]{1,0:T(8,128)S(1)} %get-tuple-element.74, f32[16,128]{1,0:T(8,128)S(1)} %get-tuple-element.73, f32[16,16]{1,0:T(8,128)S(1)} %get-tuple-element.72, ...), kind=kLoop, calls=%fused_computation.160 | loop fusion | flops 15925248 | bytes 4739400 | tf_op jit(solution)/shard_map/mul | solution.py:92
  314.7 7.6 %subtract_add_fusion.1 = (f32[16,18,16,128]{3,2,1,0:T(8,128)}, f32[16,18,16,128]{3,2,1,0:T(8,128)}, f32[16,18,16,128]{3,2,1,0:T(8,128)}, f32[16,18,16,128]{3,2,1...) fusion(f32[16,18,16,128]{3,2,1,0:T(8,128)S(1)} %add_multiply_fusion, ...), kind=kLoop, calls=%fused_computation.151 | loop fusion | flops 10027008 | bytes 18895104 | tf_op jit(solution)/shard_map/add | solution.py:50
  325.6 18.9 %conditional.7 = (f32[16,6,16,128]{3,2,1,0:T(8,128)}) conditional(s32[]{:T(128)} %bitcast.4, f32[16,6,16,128]{3,2,1,0:T(8,128)S(1)} %fusion.40, f32[16,6,16,128]{3,2,1,0:T(8,128)S(1)} %fusion.40, f32[16,6,16,128]{3,2,1,0:T(8,128)S(1)} %fusion.40, f32[16,6,16,128]{3,2,1,0:T(8,128)S(1)} %fusion.40), branch_computations={%region_13.14_spmd, %region_14.15_spmd, %region_15.16_spmd, %regio... | conditional | bytes 3145776 | solution.py:95
  327.5 17.0 %collective-permute-done.15 = f32[16,6,16,128]{3,2,1,0:T(8,128)} collective-permute-done((f32[16,6,16,128]{3,2,1,0:T(8,128)S(1)}, f32[16,6,16,128]{3,2,1,0:T(8,128)}, u32[]{:S(2)}, u32[]{:S(2)}) %collective-permute-start.15) | collective-permute-done | bytes 786464 | tf_op jit(solution)/shard_map/cond/branch_3_fun/ppermute | solution.py:20
  (61 shorter events, 85.9 us)
Async XLA Ops:
  0.0 24.8 %collective-permute-start.16 = (f32[16,6,16,128]{3,2,1,0:T(8,128)}, f32[16,6,16,128]{3,2,1,0:T(8,128)S(1)}, u32[]{:S(2)}, u32[]{:S(2)}) collective-permute-start(f32[16,6,16,128]{3,2,1,0:T(8,128)} %param.22), channel_id=1, source_target_pairs={{0,1},{1,2},{2,3},{3,4},{4,5},{5,6},{6,7},{7,8},{8,9},{9,10},{10,1... | collective-permute-start | bytes 2359304 | tf_op jit(solution)/shard_map/ppermute | solution.py:31
  1.9 28.6 %collective-permute-start.17 = (f32[16,6,16,128]{3,2,1,0:T(8,128)}, f32[16,6,16,128]{3,2,1,0:T(8,128)S(1)}, u32[]{:S(2)}, u32[]{:S(2)}) collective-permute-start(f32[16,6,16,128]{3,2,1,0:T(8,128)} %param.22), channel_id=1, source_target_pairs={{1,0},{2,1},{3,2},{4,3},{5,4},{6,5},{7,6},{8,7},{9,8},{10,9},{11,1... | collective-permute-start | bytes 2359304 | tf_op jit(solution)/shard_map/ppermute | solution.py:33
  59.4 37.8 %collective-permute-start.1 = (f32[16,6,16,128]{3,2,1,0:T(8,128)S(1)}, f32[16,6,16,128]{3,2,1,0:T(8,128)}, u32[]{:S(2)}, u32[]{:S(2)}) collective-permute-start(f32[16,6,16,128]{3,2,1,0:T(8,128)S(1)} %param.1), channel_id=1, source_target_pairs={{0,128},{32,160},{64,192},{96,224},{128,0},{160,32},{192,64},{224,... | collective-permute-start | bytes 2359304 | tf_op jit(solution)/shard_map/cond/branch_1_fun/ppermute | solution.py:20
  98.7 25.1 %collective-permute-start.18 = (f32[16,6,16,128]{3,2,1,0:T(8,128)S(1)}, f32[16,6,16,128]{3,2,1,0:T(8,128)S(1)}, u32[]{:S(2)}, u32[]{:S(2)}) collective-permute-start(f32[16,6,16,128]{3,2,1,0:T(8,128)S(1)} %subtract_select_fusion.3), channel_id=1, source_target_pairs={{0,1},{1,2},{2,3},{3,4},{4,5},{5,6},{6,7},{7,8},{8,9},{9,10},{10,1... | collective-permute-start | bytes 2359304 | tf_op jit(solution)/shard_map/ppermute | solution.py:31
  100.6 24.6 %collective-permute-start.19 = (f32[16,6,16,128]{3,2,1,0:T(8,128)S(1)}, f32[16,6,16,128]{3,2,1,0:T(8,128)S(1)}, u32[]{:S(2)}, u32[]{:S(2)}) collective-permute-start(f32[16,6,16,128]{3,2,1,0:T(8,128)S(1)} %subtract_select_fusion.3), channel_id=1, source_target_pairs={{1,0},{2,1},{3,2},{4,3},{5,4},{6,5},{7,6},{8,7},{9,8},{10,9},{11,1... | collective-permute-start | bytes 2359304 | tf_op jit(solution)/shard_map/ppermute | solution.py:33
  154.0 41.7 %collective-permute-start.4 = (f32[16,6,16,128]{3,2,1,0:T(8,128)S(1)}, f32[16,6,16,128]{3,2,1,0:T(8,128)}, u32[]{:S(2)}, u32[]{:S(2)}) collective-permute-start(f32[16,6,16,128]{3,2,1,0:T(8,128)S(1)} %param.4), channel_id=1, source_target_pairs={{0,256},{32,288},{64,320},{96,352},{128,384},{160,416},{192,448},{... | collective-permute-start | bytes 2359304 | tf_op jit(solution)/shard_map/cond/branch_0_fun/ppermute | solution.py:20
  197.2 24.7 %collective-permute-start.20 = (f32[16,6,16,128]{3,2,1,0:T(8,128)S(1)}, f32[16,6,16,128]{3,2,1,0:T(8,128)S(1)}, u32[]{:S(2)}, u32[]{:S(2)}) collective-permute-start(f32[16,6,16,128]{3,2,1,0:T(8,128)S(1)} %subtract_select_fusion.2), channel_id=1, source_target_pairs={{0,1},{1,2},{2,3},{3,4},{4,5},{5,6},{6,7},{7,8},{8,9},{9,10},{10,1... | collective-permute-start | bytes 2359304 | tf_op jit(solution)/shard_map/ppermute | solution.py:31
  199.1 22.8 %collective-permute-start.21 = (f32[16,6,16,128]{3,2,1,0:T(8,128)S(1)}, f32[16,6,16,128]{3,2,1,0:T(8,128)S(1)}, u32[]{:S(2)}, u32[]{:S(2)}) collective-permute-start(f32[16,6,16,128]{3,2,1,0:T(8,128)S(1)} %subtract_select_fusion.2), channel_id=1, source_target_pairs={{1,0},{2,1},{3,2},{4,3},{5,4},{6,5},{7,6},{8,7},{9,8},{10,9},{11,1... | collective-permute-start | bytes 2359304 | tf_op jit(solution)/shard_map/ppermute | solution.py:33
  250.8 17.9 %collective-permute-start.10 = (f32[16,6,16,128]{3,2,1,0:T(8,128)S(1)}, f32[16,6,16,128]{3,2,1,0:T(8,128)}, u32[]{:S(2)}, u32[]{:S(2)}) collective-permute-start(f32[16,6,16,128]{3,2,1,0:T(8,128)S(1)} %param.10), channel_id=1, source_target_pairs={{0,64},{32,96},{64,0},{96,32},{128,192},{160,224},{192,128},{224,1... | collective-permute-start | bytes 2359304 | tf_op jit(solution)/shard_map/cond/branch_2_fun/ppermute | solution.py:20
  270.1 24.7 %collective-permute-start.22 = (f32[16,6,16,128]{3,2,1,0:T(8,128)S(1)}, f32[16,6,16,128]{3,2,1,0:T(8,128)S(1)}, u32[]{:S(2)}, u32[]{:S(2)}) collective-permute-start(f32[16,6,16,128]{3,2,1,0:T(8,128)S(1)} %subtract_select_fusion.1), channel_id=1, source_target_pairs={{0,1},{1,2},{2,3},{3,4},{4,5},{5,6},{6,7},{7,8},{8,9},{9,10},{10,1... | collective-permute-start | bytes 2359304 | tf_op jit(solution)/shard_map/ppermute | solution.py:31
  272.1 24.6 %collective-permute-start.23 = (f32[16,6,16,128]{3,2,1,0:T(8,128)S(1)}, f32[16,6,16,128]{3,2,1,0:T(8,128)S(1)}, u32[]{:S(2)}, u32[]{:S(2)}) collective-permute-start(f32[16,6,16,128]{3,2,1,0:T(8,128)S(1)} %subtract_select_fusion.1), channel_id=1, source_target_pairs={{1,0},{2,1},{3,2},{4,3},{5,4},{6,5},{7,6},{8,7},{9,8},{10,9},{11,1... | collective-permute-start | bytes 2359304 | tf_op jit(solution)/shard_map/ppermute | solution.py:33
  325.6 18.9 %collective-permute-start.15 = (f32[16,6,16,128]{3,2,1,0:T(8,128)S(1)}, f32[16,6,16,128]{3,2,1,0:T(8,128)}, u32[]{:S(2)}, u32[]{:S(2)}) collective-permute-start(f32[16,6,16,128]{3,2,1,0:T(8,128)S(1)} %param.15), channel_id=1, source_target_pairs={{0,32},{32,0},{64,96},{96,64},{128,160},{160,128},{192,224},{224,1... | collective-permute-start | bytes 2359304 | tf_op jit(solution)/shard_map/cond/branch_3_fun/ppermute | solution.py:20
where the time goes:
time: 348 us; the launch traced here: 347 us
  waiting for transfers between devices  146 us (42%)
  other arithmetic  133 us (38%)
  starting transfers between devices  55.1 us (16%)
  between operations  7.96 us (2%)
  local copies, waits for them, and re-layouts  4.56 us (1%)
    ppermute x4, waiting for transfers between devices, partner(): return lax.ppermute(value, axis, pairs)  100 us
    mul x24, other arithmetic, local(): wide = substep(wide, drift_x, drift_y, drift_z) * inside  84.2 us
    ppermute x4, waiting for transfers between devices, extended(): lax.ppermute(tail, axis, [(i, (i + 1) % count) for i in range(ends)])  38.4 us
    ppermute x4, starting transfers between devices, extended(): lax.ppermute(head, axis, [((i + 1) % count, i) for i in range(ends)])  31.3 us
    add x4, other arithmetic, along(): upper - 2.0 * field + lower  30.5 us
    ppermute x4, starting transfers between devices, partner(): return lax.ppermute(value, axis, pairs)  16.1 us
    ppermute x4, waiting for transfers between devices, extended(): lax.ppermute(head, axis, [((i + 1) % count, i) for i in range(ends)])  7.68 us
    ppermute x4, starting transfers between devices, extended(): lax.ppermute(tail, axis, [(i, (i + 1) % count) for i in range(ends)])  7.67 us
  transfers between devices with their start and end apart: 12, of which 10 were waited for; matrix products, arithmetic and copies ran while one was open for 4% of the time, Pallas kernels for 0%

commit v1 on v0

v1 whole, which is shorter than its diff:
```python
from functools import partial

import jax
import jax.numpy as jnp
from jax import lax
from jax.experimental import pallas as pl
from jax.experimental.pallas import tpu as pltpu
from jax.sharding import PartitionSpec as P

STATE_BITS = 8
BLOCKS = 4
SUBSTEPS = 6
DIFF = 1.0
TIME_STEP = 0.15
SIDE = TIME_STEP * DIFF
HALF = 0.5 * TIME_STEP
CENTRE = 1.0 - 6.0 * TIME_STEP * DIFF


def split_rows(ref, state, layer):
    even = ref[state, layer, pl.ds(0, 8, stride=2), :]
    odd = ref[state, layer, pl.ds(1, 8, stride=2), :]
    return even, odd


def evolve_state(state, own, near, far, lev, ux, vx, core, first_x, total_x, width, store):
    size_y, size_z = own.shape[2], own.shape[3]
    shape = (8, size_z)
    lx = jnp.broadcast_to(lev[state, 0:1, :], shape)
    ly = jnp.broadcast_to(lev[state, 1:2, :], shape)
    lz = jnp.broadcast_to(lev[state, 2:3, :], shape)
    span = width + 2 * SUBSTEPS
    for c in range(1, span - 1):
        cell = first_x - SUBSTEPS + c
        inside = jnp.where((cell >= 0) & (cell < total_x), 1.0, 0.0)
        above = (cell.astype(jnp.float32) + 1.5) / total_x
        below = (cell.astype(jnp.float32) - 0.5) / total_x
        ux[c] = (SIDE - HALF * (lx - above)) * inside
        vx[c] = (SIDE + HALF * (lx - below)) * inside
    row = lax.broadcasted_iota(jnp.int32, shape, 0)
    col = lax.broadcasted_iota(jnp.int32, shape, 1)
    y_even = (2 * row).astype(jnp.float32)
    zc = col.astype(jnp.float32)
    ue = SIDE - HALF * (ly - (y_even + 1.5) / size_y)
    ve = jnp.where(row == 0, 0.0, SIDE + HALF * (ly - (y_even - 0.5) / size_y))
    uo = jnp.where(row == 7, 0.0, SIDE - HALF * (ly - (y_even + 2.5) / size_y))
    vo = SIDE + HALF * (ly - (y_even + 0.5) / size_y)
    uz = jnp.where(col == size_z - 1, 0.0, SIDE - HALF * (lz - (zc + 1.5) / size_z))
    vz = jnp.where(col == 0, 0.0, SIDE + HALF * (lz - (zc - 0.5) / size_z))

    is_low = core == 0
    field = []
    for c in range(width):
        a, b = split_rows(near, state, c), split_rows(far, state, c)
        field.append(tuple(jnp.where(is_low, q, p) for p, q in zip(a, b)))
    for c in range(width):
        field.append(split_rows(own, state, c))
    for c in range(width):
        a, b = split_rows(near, state, c), split_rows(far, state, c)
        field.append(tuple(jnp.where(is_low, p, q) for p, q in zip(a, b)))

    for step in range(SUBSTEPS):
        fresh = []
        base = step + 1
        for i in range(1, len(field) - 1):
            c = base + i - 1
            even, odd = field[i]
            u, v = ux[c], vx[c]
            new = []
            for k, mid in enumerate((even, odd)):
                up, down = field[i + 1][k], field[i - 1][k]
                if k == 0:
                    y_part = ue * odd + ve * pltpu.roll(odd, 1, 0)
                else:
                    y_part = uo * pltpu.roll(even, 7, 0) + vo * even
                z_part = uz * pltpu.roll(mid, size_z - 1, 1) + vz * pltpu.roll(mid, 1, 1)
                x_part = u * up + v * down
                new.append((CENTRE * mid + x_part) + (y_part + z_part))
            fresh.append(tuple(new))
        field = fresh
    for c in range(width):
        store(c, field[c][0], field[c][1])


def switch_factors(first_x, layer, total_x, on, off, shape):
    u = (jnp.full(shape, first_x + layer, jnp.int32).astype(jnp.float32) + 0.5) / total_x
    act = on * (0.1 + u * u / (0.09 + u * u))
    rate = act + off
    return act / rate, jnp.exp(-rate)


def block_kernel(block, order, on_rate, off_rate, own, near, far, lev, out, ux, vx):
    count, width, size_y, size_z = own.shape
    place = lax.axis_index("prot")
    total_x = width * lax.axis_size("prot")
    first_x = place * width
    core = lax.rem(place, 2)

    def one(state, carry):
        def store(c, even, odd):
            out[state, c, pl.ds(0, 8, stride=2), :] = even
            out[state, c, pl.ds(1, 8, stride=2), :] = odd

        evolve_state(state, own, near, far, lev, ux, vx, core, first_x, total_x, width, store)
        return carry

    lax.fori_loop(0, count, one, 0)

    gene = order[block]
    on, off = on_rate[STATE_BITS - 1 - gene], off_rate[STATE_BITS - 1 - gene]
    bit = count.bit_length() - 2 - gene
    stride = jnp.left_shift(1, bit)
    for c in range(width):
        share, decay = switch_factors(first_x, c, total_x, on, off, (size_y, size_z))

        def pair(k, carry, c=c, share=share, decay=decay):
            low = jnp.bitwise_and(k, stride - 1)
            s = 2 * (k - low) + low
            t = s + stride
            qs, qt = out[s, c], out[t, c]
            total = qs + qt
            part = share * total
            high = part + (qt - part) * decay
            out[t, c] = high
            out[s, c] = total - high
            return carry

        lax.fori_loop(0, count // 2, pair, 0, unroll=True)


def run_block(block, order, on_rate, off_rate, own, near, far, lev):
    smem = pl.BlockSpec(memory_space=pltpu.SMEM)
    vmem = pl.BlockSpec(memory_space=pltpu.VMEM)
    span = own.shape[1] + 2 * SUBSTEPS
    updates = own.size * 11
    return pl.pallas_call(
        partial(block_kernel, block),
        out_shape=jax.ShapeDtypeStruct(own.shape, jnp.float32),
        in_specs=[smem] * 3 + [vmem] * 4,
        out_specs=vmem,
        scratch_shapes=[pltpu.VMEM((span, 8, own.shape[3]), jnp.float32)] * 2,
        compiler_params=pltpu.CompilerParams(vmem_limit_bytes=32 * 1024 * 1024),
        cost_estimate=pl.CostEstimate(flops=updates * 14, bytes_accessed=own.size * 16, transcendentals=0),
        name=f"block{block}",
    )(order, on_rate, off_rate, own, near, far, lev)


def local(density, levels, rate_index, on_rate, off_rate, gene_order):
    count, width, size_y, size_z = density.shape
    size = lax.axis_size("prot")
    onehot = rate_index[:, :, None] == jnp.arange(levels.shape[0], dtype=jnp.int32)[None, None, :]
    level_of = jnp.sum(jnp.where(onehot, levels[None, None, :], 0.0), axis=-1)
    rows = jnp.concatenate([level_of, jnp.zeros((count, 5), jnp.float32)], axis=1)
    rows = jnp.broadcast_to(rows[:, :, None], (count, 8, size_z))
    both = jnp.concatenate([density.reshape(count, width * size_y, size_z), rows], axis=1)
    both = lax.all_to_all(both, "gene", 0, 0, tiled=True)
    field = both[:, : width * size_y].reshape(density.shape)
    lev = both[:, width * size_y :]
    inner = [(i, i ^ 1) for i in range(size)]
    outer = [(i, i + 1) for i in range(1, size - 1, 2)] + [(i + 1, i) for i in range(1, size - 1, 2)]
    for block in range(BLOCKS):
        far = lax.ppermute(field, "prot", outer)
        near = lax.ppermute(field, "prot", inner)
        field = run_block(block, gene_order, on_rate, off_rate, field, near, far, lev)
    return lax.all_to_all(field, "gene", 0, 0, tiled=True)


def solution(mesh):
    in_specs = (P("gene", "prot", None, None), P(), P("gene", None), P(), P(), P())
    out_specs = P("gene", "prot", None, None)
    return jax.shard_map(local, mesh=mesh, in_specs=in_specs, out_specs=out_specs, check_vma=False)
```

time: 348 us -> 196 us (0.56)
  the two profiles are of different devices: /device:TPU:4 before, /device:TPU:2 now
where the time goes in v1:
time: 196 us; the launch traced here: 195 us
  blocking collectives  69.5 us (35%)
  waiting for transfers between devices  52.1 us (27%)
  starting transfers between devices  36.1 us (18%)
  Pallas kernels  34.4 us (18%)
  other arithmetic  1.98 us (1%)
    ppermute x4, waiting for transfers between devices, local(): far = lax.ppermute(field, 'prot', outer)  52.1 us
    all_to_all x1, blocking collectives, local(): return lax.all_to_all(field, 'gene', 0, 0, tiled=True)  36.2 us
    pallas_call x4, Pallas kernels, run_block(): pl.pallas_call(partial(block_kernel, block), out_shape=jax.ShapeDtypeStru...  34.4 us
    all_to_all x1, blocking collectives, local(): both = lax.all_to_all(both, 'gene', 0, 0, tiled=True)  33.3 us
    ppermute x4, starting transfers between devices, local(): far = lax.ppermute(field, 'prot', outer)  26 us
    ppermute x4, starting transfers between devices, local(): near = lax.ppermute(field, 'prot', inner)  10 us
  transfers between devices with their start and end apart: 8, of which 4 were waited for; matrix products, arithmetic and copies ran while one was open for 0% of the time, Pallas kernels for 0%

profile of v1, /device:TPU:2, one launch (start us, length us, event | category | flops | bytes accessed | tf_op | source)
XLA Modules:
  0.0 195.4 jit_solution(7443963415612557132)
XLA Ops:
  0.0 0.8 select_reduce_fusion
  0.8 0.1 copy.9
  0.9 0.1 broadcast_in_dim.24
  1.0 1.2 pad_maximum_fusion
  2.2 33.3 %all_to_all.10 = f32[16,104,128]{2,1,0:T(8,128)S(1)} all-to-all(f32[16,104,128]{2,1,0:T(8,128)S(1)} %pad_maximum_fusion), channel_id=1, replica_groups=mesh['gene'=16,'prot'=32] {'gene'}, dimensions={0} | all-to-all | bytes 1703936 | tf_op jit(solution)/shard_map/all_to_all | solution.py:156
  35.5 0.1 slice.8
  35.5 0.0 copy-start
  35.6 0.0 copy-start.1
  35.6 0.0 copy-start.2
  35.6 8.0 %collective-permute-start.1 = (f32[16,6,16,128]{3,2,1,0:T(8,128)S(1)}, f32[16,6,16,128]{3,2,1,0:T(8,128)S(1)}, u32[]{:S(2)}, u32[]{:S(2)}) collective-permute-start(f32[16,6,16,128]{3,2,1,0:T(8,128)S(1)} %bitcast.2), channel_id=1, source_target_pairs={{1,2},{3,4},{5,6},{7,8},{9,10},{11,12},{13,14},{15,16},{17,18},{19... | collective-permute-start | bytes 2359304 | tf_op jit(solution)/shard_map/ppermute | solution.py:162
  43.6 1.9 collective-permute-start
  45.6 13.7 %collective-permute-done.1.far = f32[16,6,16,128]{3,2,1,0:T(8,128)S(1)} collective-permute-done((f32[16,6,16,128]{3,2,1,0:T(8,128)S(1)}, f32[16,6,16,128]{3,2,1,0:T(8,128)S(1)}, u32[]{:S(2)}, u32[]{:S(2)}) %collective-permute-start.1) | collective-permute-done | bytes 786464 | tf_op jit(solution)/shard_map/ppermute | solution.py:162
  59.2 0.0 collective-permute-done.near
  59.2 0.0 copy-done
  59.3 8.6 %block0.1.own = f32[16,6,16,128]{3,2,1,0:T(8,128)S(1)} custom-call(s32[4]{0:T(128)S(1)} %copy-done, f32[8]{0:T(128)S(1)} %copy-done.1, f32[8]{0:T(128)S(1)} %copy-done.2, f32[16,6,16,128]{3,2,1,0:T(8,128)S(1)} %bitcast.4, f32[16,6,16,128]{3,2,1,0:T(8,128)S(1)} %collective-permute-done.near, f32[16,6,16,128]{3,2,1,0:T(8,128)S(1)} %collective-permute-done.1.far, ...), custom_call_target="tpu_custom_call" | custom-call | flops 30277632 | bytes 3145728 | tf_op jit(solution)/shard_map/block0/pallas_call | solution.py:136
  67.9 6.8 %collective-permute-start.3 = (f32[16,6,16,128]{3,2,1,0:T(8,128)S(1)}, f32[16,6,16,128]{3,2,1,0:T(8,128)S(1)}, u32[]{:S(2)}, u32[]{:S(2)}) collective-permute-start(f32[16,6,16,128]{3,2,1,0:T(8,128)S(1)} %block0.1.own), channel_id=1, source_target_pairs={{1,2},{3,4},{5,6},{7,8},{9,10},{11,12},{13,14},{15,16},{17,18},{19... | collective-permute-start | bytes 2359304 | tf_op jit(solution)/shard_map/ppermute | solution.py:162
  74.7 1.9 collective-permute-start.2
  76.6 11.8 %collective-permute-done.3.far = f32[16,6,16,128]{3,2,1,0:T(8,128)S(1)} collective-permute-done((f32[16,6,16,128]{3,2,1,0:T(8,128)S(1)}, f32[16,6,16,128]{3,2,1,0:T(8,128)S(1)}, u32[]{:S(2)}, u32[]{:S(2)}) %collective-permute-start.3) | collective-permute-done | bytes 786464 | tf_op jit(solution)/shard_map/ppermute | solution.py:162
  88.5 0.0 collective-permute-done.2.near
  88.5 8.6 %block1.1.own = f32[16,6,16,128]{3,2,1,0:T(8,128)S(1)} custom-call(s32[4]{0:T(128)S(1)} %copy-done, f32[8]{0:T(128)S(1)} %copy-done.1, f32[8]{0:T(128)S(1)} %copy-done.2, f32[16,6,16,128]{3,2,1,0:T(8,128)S(1)} %block0.1.own, f32[16,6,16,128]{3,2,1,0:T(8,128)S(1)} %collective-permute-done.2.near, f32[16,6,16,128]{3,2,1,0:T(8,128)S(1)} %collective-permute-done.3.far, ...), custom_call_target="tpu_custom_call" | custom-call | flops 30277632 | bytes 3145728 | tf_op jit(solution)/shard_map/block1/pallas_call | solution.py:136
  97.1 6.8 %collective-permute-start.5 = (f32[16,6,16,128]{3,2,1,0:T(8,128)S(1)}, f32[16,6,16,128]{3,2,1,0:T(8,128)S(1)}, u32[]{:S(2)}, u32[]{:S(2)}) collective-permute-start(f32[16,6,16,128]{3,2,1,0:T(8,128)S(1)} %block1.1.own), channel_id=1, source_target_pairs={{1,2},{3,4},{5,6},{7,8},{9,10},{11,12},{13,14},{15,16},{17,18},{19... | collective-permute-start | bytes 2359304 | tf_op jit(solution)/shard_map/ppermute | solution.py:162
  104.0 1.9 collective-permute-start.4
  105.9 10.4 %collective-permute-done.5.far = f32[16,6,16,128]{3,2,1,0:T(8,128)S(1)} collective-permute-done((f32[16,6,16,128]{3,2,1,0:T(8,128)S(1)}, f32[16,6,16,128]{3,2,1,0:T(8,128)S(1)}, u32[]{:S(2)}, u32[]{:S(2)}) %collective-permute-start.5) | collective-permute-done | bytes 786464 | tf_op jit(solution)/shard_map/ppermute | solution.py:162
  116.2 0.0 collective-permute-done.4.near
  116.2 8.6 %block2.1.own = f32[16,6,16,128]{3,2,1,0:T(8,128)S(1)} custom-call(s32[4]{0:T(128)S(1)} %copy-done, f32[8]{0:T(128)S(1)} %copy-done.1, f32[8]{0:T(128)S(1)} %copy-done.2, f32[16,6,16,128]{3,2,1,0:T(8,128)S(1)} %block1.1.own, f32[16,6,16,128]{3,2,1,0:T(8,128)S(1)} %collective-permute-done.4.near, f32[16,6,16,128]{3,2,1,0:T(8,128)S(1)} %collective-permute-done.5.far, ...), custom_call_target="tpu_custom_call" | custom-call | flops 30277632 | bytes 3145728 | tf_op jit(solution)/shard_map/block2/pallas_call | solution.py:136
  124.9 4.3 %collective-permute-start.7 = (f32[16,6,16,128]{3,2,1,0:T(8,128)S(1)}, f32[16,6,16,128]{3,2,1,0:T(8,128)S(1)}, u32[]{:S(2)}, u32[]{:S(2)}) collective-permute-start(f32[16,6,16,128]{3,2,1,0:T(8,128)S(1)} %block2.1.own), channel_id=1, source_target_pairs={{1,2},{3,4},{5,6},{7,8},{9,10},{11,12},{13,14},{15,16},{17,18},{19... | collective-permute-start | bytes 2359304 | tf_op jit(solution)/shard_map/ppermute | solution.py:162
  129.2 4.3 %collective-permute-start.6 = (f32[16,6,16,128]{3,2,1,0:T(8,128)S(1)}, f32[16,6,16,128]{3,2,1,0:T(8,128)S(1)}, u32[]{:S(2)}, u32[]{:S(2)}) collective-permute-start(f32[16,6,16,128]{3,2,1,0:T(8,128)S(1)} %block2.1.own), channel_id=1, source_target_pairs={{0,1},{1,0},{2,3},{3,2},{4,5},{5,4},{6,7},{7,6},{8,9},{9,8},{10,11... | collective-permute-start | bytes 2359304 | tf_op jit(solution)/shard_map/ppermute | solution.py:163
  133.4 16.3 %collective-permute-done.7.far = f32[16,6,16,128]{3,2,1,0:T(8,128)S(1)} collective-permute-done((f32[16,6,16,128]{3,2,1,0:T(8,128)S(1)}, f32[16,6,16,128]{3,2,1,0:T(8,128)S(1)}, u32[]{:S(2)}, u32[]{:S(2)}) %collective-permute-start.7) | collective-permute-done | bytes 786464 | tf_op jit(solution)/shard_map/ppermute | solution.py:162
  149.7 0.0 collective-permute-done.6.near
  149.7 8.6 %block3.1 = f32[16,6,16,128]{3,2,1,0:T(8,128)S(1)} custom-call(s32[4]{0:T(128)S(1)} %copy-done, f32[8]{0:T(128)S(1)} %copy-done.1, f32[8]{0:T(128)S(1)} %copy-done.2, f32[16,6,16,128]{3,2,1,0:T(8,128)S(1)} %block2.1.own, f32[16,6,16,128]{3,2,1,0:T(8,128)S(1)} %collective-permute-done.6.near, f32[16,6,16,128]{3,2,1,0:T(8,128)S(1)} %collective-permute-done.7.far, ...), custom_call_target="tpu_custom_call" | custom-call | flops 30277632 | bytes 3145728 | tf_op jit(solution)/shard_map/block3/pallas_call | solution.py:136
  158.3 36.2 %all_to_all.11 = f32[16,6,16,128]{3,2,1,0:T(8,128)S(1)} all-to-all(f32[16,6,16,128]{3,2,1,0:T(8,128)S(1)} %block3.1), channel_id=1, replica_groups=mesh['gene'=16,'prot'=32] {'gene'}, dimensions={0} | all-to-all | bytes 1572864 | tf_op jit(solution)/shard_map/all_to_all | solution.py:165
  194.5 0.9 copy.11
  (4 shorter events, 0.0 us)
Async XLA Ops:
  35.5 23.7 %copy-start = (s32[4]{0:T(128)S(1)}, s32[4]{0:T(128)}, u32[]{:S(2)}) copy-start(s32[4]{0:T(128)} %order.7) | copy-start | bytes 52
  35.6 23.7 %copy-start.1 = (f32[8]{0:T(128)S(1)}, f32[8]{0:T(128)}, u32[]{:S(2)}) copy-start(f32[8]{0:T(128)} %on_rate.7) | copy-start | bytes 100
  35.6 23.7 %copy-start.2 = (f32[8]{0:T(128)S(1)}, f32[8]{0:T(128)}, u32[]{:S(2)}) copy-start(f32[8]{0:T(128)} %off_rate.7) | copy-start | bytes 100
  35.6 23.7 %collective-permute-start.1 = (f32[16,6,16,128]{3,2,1,0:T(8,128)S(1)}, f32[16,6,16,128]{3,2,1,0:T(8,128)S(1)}, u32[]{:S(2)}, u32[]{:S(2)}) collective-permute-start(f32[16,6,16,128]{3,2,1,0:T(8,128)S(1)} %bitcast.2), channel_id=1, source_target_pairs={{1,2},{3,4},{5,6},{7,8},{9,10},{11,12},{13,14},{15,16},{17,18},{19... | collective-permute-start | bytes 2359304 | tf_op jit(solution)/shard_map/ppermute | solution.py:162
  43.6 15.6 %collective-permute-start = (f32[16,6,16,128]{3,2,1,0:T(8,128)S(1)}, f32[16,6,16,128]{3,2,1,0:T(8,128)S(1)}, u32[]{:S(2)}, u32[]{:S(2)}) collective-permute-start(f32[16,6,16,128]{3,2,1,0:T(8,128)S(1)} %bitcast.3), channel_id=1, source_target_pairs={{0,1},{1,0},{2,3},{3,2},{4,5},{5,4},{6,7},{7,6},{8,9},{9,8},{10,11... | collective-permute-start | bytes 2359304 | tf_op jit(solution)/shard_map/ppermute | solution.py:163
  67.9 20.6 %collective-permute-start.3 = (f32[16,6,16,128]{3,2,1,0:T(8,128)S(1)}, f32[16,6,16,128]{3,2,1,0:T(8,128)S(1)}, u32[]{:S(2)}, u32[]{:S(2)}) collective-permute-start(f32[16,6,16,128]{3,2,1,0:T(8,128)S(1)} %block0.1.own), channel_id=1, source_target_pairs={{1,2},{3,4},{5,6},{7,8},{9,10},{11,12},{13,14},{15,16},{17,18},{19... | collective-permute-start | bytes 2359304 | tf_op jit(solution)/shard_map/ppermute | solution.py:162
  74.7 13.8 %collective-permute-start.2 = (f32[16,6,16,128]{3,2,1,0:T(8,128)S(1)}, f32[16,6,16,128]{3,2,1,0:T(8,128)S(1)}, u32[]{:S(2)}, u32[]{:S(2)}) collective-permute-start(f32[16,6,16,128]{3,2,1,0:T(8,128)S(1)} %block0.1.own), channel_id=1, source_target_pairs={{0,1},{1,0},{2,3},{3,2},{4,5},{5,4},{6,7},{7,6},{8,9},{9,8},{10,11... | collective-permute-start | bytes 2359304 | tf_op jit(solution)/shard_map/ppermute | solution.py:163
  97.1 19.1 %collective-permute-start.5 = (f32[16,6,16,128]{3,2,1,0:T(8,128)S(1)}, f32[16,6,16,128]{3,2,1,0:T(8,128)S(1)}, u32[]{:S(2)}, u32[]{:S(2)}) collective-permute-start(f32[16,6,16,128]{3,2,1,0:T(8,128)S(1)} %block1.1.own), channel_id=1, source_target_pairs={{1,2},{3,4},{5,6},{7,8},{9,10},{11,12},{13,14},{15,16},{17,18},{19... | collective-permute-start | bytes 2359304 | tf_op jit(solution)/shard_map/ppermute | solution.py:162
  104.0 12.3 %collective-permute-start.4 = (f32[16,6,16,128]{3,2,1,0:T(8,128)S(1)}, f32[16,6,16,128]{3,2,1,0:T(8,128)S(1)}, u32[]{:S(2)}, u32[]{:S(2)}) collective-permute-start(f32[16,6,16,128]{3,2,1,0:T(8,128)S(1)} %block1.1.own), channel_id=1, source_target_pairs={{0,1},{1,0},{2,3},{3,2},{4,5},{5,4},{6,7},{7,6},{8,9},{9,8},{10,11... | collective-permute-start | bytes 2359304 | tf_op jit(solution)/shard_map/ppermute | solution.py:163
  124.9 24.8 %collective-permute-start.7 = (f32[16,6,16,128]{3,2,1,0:T(8,128)S(1)}, f32[16,6,16,128]{3,2,1,0:T(8,128)S(1)}, u32[]{:S(2)}, u32[]{:S(2)}) collective-permute-start(f32[16,6,16,128]{3,2,1,0:T(8,128)S(1)} %block2.1.own), channel_id=1, source_target_pairs={{1,2},{3,4},{5,6},{7,8},{9,10},{11,12},{13,14},{15,16},{17,18},{19... | collective-permute-start | bytes 2359304 | tf_op jit(solution)/shard_map/ppermute | solution.py:162
  129.2 20.5 %collective-permute-start.6 = (f32[16,6,16,128]{3,2,1,0:T(8,128)S(1)}, f32[16,6,16,128]{3,2,1,0:T(8,128)S(1)}, u32[]{:S(2)}, u32[]{:S(2)}) collective-permute-start(f32[16,6,16,128]{3,2,1,0:T(8,128)S(1)} %block2.1.own), channel_id=1, source_target_pairs={{0,1},{1,0},{2,3},{3,2},{4,5},{5,4},{6,7},{7,6},{8,9},{9,8},{10,11... | collective-permute-start | bytes 2359304 | tf_op jit(solution)/shard_map/ppermute | solution.py:163

commit v2 on v1

v2 whole, which is shorter than its diff:
```python
from functools import partial

import jax
import jax.numpy as jnp
from jax import lax
from jax.experimental import pallas as pl
from jax.experimental.pallas import tpu as pltpu
from jax.sharding import PartitionSpec as P

STATE_BITS = 8
BLOCKS = 4
SUBSTEPS = 6
DIFF = 1.0
TIME_STEP = 0.15
SIDE = TIME_STEP * DIFF
HALF = 0.5 * TIME_STEP
ROWS = 8
CENTRE = 1.0 - 6.0 * TIME_STEP * DIFF


def switch_factors(first_x, layer, total_x, on, off, shape):
    u = (jnp.full(shape, first_x + layer, jnp.int32).astype(jnp.float32) + 0.5) / total_x
    act = on * (0.1 + u * u / (0.09 + u * u))
    rate = act + off
    return act / rate, jnp.exp(-rate)


def spread(place, bit, value):
    low = jnp.bitwise_and(place, jnp.left_shift(1, bit) - 1)
    return 2 * (place - low) + low + jnp.left_shift(value, bit)


def swap_bits(value):
    row = lax.broadcasted_iota(jnp.int32, value.shape, 0)
    col = lax.broadcasted_iota(jnp.int32, value.shape, 1)
    lanes = value.shape[1]
    for k in (1, 2, 4):
        row_set, col_set = jnp.bitwise_and(row, k) != 0, jnp.bitwise_and(col, k) != 0
        down = pltpu.roll(pltpu.roll(value, k, 0), lanes - k, 1)
        up = pltpu.roll(pltpu.roll(value, ROWS - k, 0), k, 1)
        value = jnp.where(row_set == col_set, value, jnp.where(row_set, down, up))
    return value


def entry_kernel(width, size_y, order, on_rate, off_rate, both, low, high, x_table, y_table, z_table, mix_table, packed, turned):
    last_bit = BLOCKS - 1 - order[BLOCKS - 1]
    layer_rows = width * size_y
    size_z = both.shape[2]
    count = both.shape[0] // 2
    shape = (ROWS, size_z)
    place = lax.axis_index("prot")
    total_x = width * lax.axis_size("prot")
    first_x = place * width
    row = lax.broadcasted_iota(jnp.int32, shape, 0)
    col = lax.broadcasted_iota(jnp.int32, shape, 1)
    lane_state = jnp.bitwise_and(lax.broadcasted_iota(jnp.int32, (1, size_z), 1), count - 1)
    for chunk in range(2):
        for k in range(count):
            packed[chunk, pl.ds(k * layer_rows, layer_rows), :] = both[spread(k, last_bit, chunk), 0:layer_rows, :]

    def layer(x, carry):
        for chunk in range(2):
            for y in range(size_y):
                turned[chunk, pl.ds(y * ROWS, ROWS), :] = swap_bits(
                    packed[chunk, pl.ds(x * size_y + y, count, stride=layer_rows), :]
                )
        for chunk, out in enumerate((low, high)):
            for q in range(2 * ROWS):
                out[x, q] = turned[chunk, pl.ds((q % 2) * ROWS + q // 2, ROWS, stride=2 * ROWS), :]
        return carry

    lax.fori_loop(0, width, layer, 0)
    for chunk in range(2):
        lines = []
        for r in range(3):
            line = jnp.zeros((1, size_z), jnp.float32)
            for k in range(count):
                line = jnp.where(lane_state == k, both[spread(k, last_bit, chunk), layer_rows + r : layer_rows + r + 1, :], line)
            lines.append(jnp.broadcast_to(line, shape))
        lx, ly, lz = lines
        for c in range(x_table.shape[2]):
            cell = first_x - SUBSTEPS + c
            inside = jnp.where((cell >= 0) & (cell < total_x), 1.0, 0.0)
            centre = jnp.full(shape, cell, jnp.int32).astype(jnp.float32)
            x_table[chunk, 0, c] = (SIDE - HALF * (lx - (centre + 1.5) / total_x)) * inside
            x_table[chunk, 1, c] = (SIDE + HALF * (lx - (centre - 0.5) / total_x)) * inside
        y_even = (2 * row).astype(jnp.float32)
        y_table[chunk, 0] = SIDE - HALF * (ly - (y_even + 1.5) / size_y)
        y_table[chunk, 1] = jnp.where(row == 0, 0.0, SIDE + HALF * (ly - (y_even - 0.5) / size_y))
        y_table[chunk, 2] = jnp.where(row == ROWS - 1, 0.0, SIDE - HALF * (ly - (y_even + 2.5) / size_y))
        y_table[chunk, 3] = SIDE + HALF * (ly - (y_even + 0.5) / size_y)
        for j in range(ROWS):
            z = jnp.bitwise_and(col, -ROWS) + j
            zc = z.astype(jnp.float32)
            z_table[chunk, 0, j] = jnp.where(z == size_z - 1, 0.0, SIDE - HALF * (lz - (zc + 1.5) / size_z))
            z_table[chunk, 1, j] = jnp.where(z == 0, 0.0, SIDE + HALF * (lz - (zc - 0.5) / size_z))
    for block in range(BLOCKS):
        bit = STATE_BITS - 1 - order[block]
        for c in range(width):
            share, decay = switch_factors(first_x, c, total_x, on_rate[bit], off_rate[bit], shape)
            mix_table[block, 0, c] = share
            mix_table[block, 1, c] = decay


def enter(scalars, both, width, size_y):
    lanes = both.shape[2]
    smem = pl.BlockSpec(memory_space=pltpu.SMEM)
    vmem = pl.BlockSpec(memory_space=pltpu.VMEM)
    tile = (ROWS, lanes)
    chunk = (width, 2 * ROWS) + tile
    dims = [chunk, chunk, (2, 2, width + 2 * SUBSTEPS) + tile, (2, 4) + tile, (2, 2, ROWS) + tile, (BLOCKS, 2, width) + tile]
    return pl.pallas_call(
        partial(entry_kernel, width, size_y),
        out_shape=tuple(jax.ShapeDtypeStruct(d, jnp.float32) for d in dims),
        in_specs=[smem] * 3 + [vmem],
        out_specs=(vmem,) * len(dims),
        scratch_shapes=[
            pltpu.VMEM((2, ROWS * width * size_y, lanes), jnp.float32),
            pltpu.VMEM((2, size_y * ROWS, lanes), jnp.float32),
        ],
        compiler_params=pltpu.CompilerParams(vmem_limit_bytes=32 * 1024 * 1024),
        name="enter",
    )(*scalars, both)


def block_kernel(mode, block, chunk, order, own, left, right, x_table, y_table, z_table, mix_table, *rest):
    rest = list(rest)
    other = rest.pop(0) if mode == "join" else None
    out, first, second = rest[:3]
    width, parts, rows, lanes = own.shape
    size_y, count = 2 * rows, ROWS
    shape = (rows, lanes)
    span = width + 2 * SUBSTEPS
    last_bit = BLOCKS - 1 - order[BLOCKS - 1]
    bit = BLOCKS - 1 - order[block]
    inner_bit = jnp.where(bit > last_bit, bit - 1, bit)
    ue, ve, uo, vo = (y_table[chunk, k] for k in range(4))
    col = lax.broadcasted_iota(jnp.int32, shape, 1)
    is_high = jnp.bitwise_and(jnp.right_shift(col, inner_bit), 1) == 1
    apart = jnp.left_shift(1, inner_bit)

    def finish(c, q, value):
        if mode != "inside":
            return value
        mate = jnp.where(is_high, pltpu.roll(value, apart, 1), pltpu.roll(value, lanes - apart, 1))
        total = value + mate
        part = mix_table[block, 0, c] * total
        up = part + (jnp.where(is_high, value, mate) - part) * mix_table[block, 1, c]
        return jnp.where(is_high, up, total - up)

    def given(c, q):
        return (left, own, right)[c // width][c % width, q]

    read = given
    for step in range(SUBSTEPS):
        target = (first, second)[step % 2]
        final = step == SUBSTEPS - 1
        for c in range(step + 1, span - 1 - step):
            u, v = x_table[chunk, 0, c], x_table[chunk, 1, c]
            mids = [read(c, q) for q in range(parts)]
            sums = [CENTRE * mids[q] + (u * read(c + 1, q) + v * read(c - 1, q)) for q in range(parts)]
            fresh = []
            for q in range(parts):
                j, odd = q // 2, q % 2
                pair = mids[q ^ 1]
                if odd:
                    y_part = uo * pltpu.roll(pair, rows - 1, 0) + vo * pair
                else:
                    y_part = ue * pair + ve * pltpu.roll(pair, 1, 0)
                z_up = mids[q + 2] if q + 2 < parts else pltpu.roll(mids[odd], lanes - ROWS, 1)
                z_down = mids[q - 2] if q >= 2 else pltpu.roll(mids[parts - 2 + odd], ROWS, 1)
                z_part = z_table[chunk, 0, j] * z_up + z_table[chunk, 1, j] * z_down
                fresh.append(sums[q] + (y_part + z_part))
            for q in range(parts):
                if final and mode != "join":
                    out[c - width, q] = finish(c - width, q, fresh[q])
                else:
                    target[c, q] = fresh[q]
        read = lambda c, q, ref=target: ref[c, q]
    if mode != "join":
        return
    source = target
    packed, turned = rest[3:]
    layer_rows = width * size_y

    def leave(c, carry):
        share, decay = mix_table[block, 0, c], mix_table[block, 1, c]
        for q in range(parts):
            low, high = other[c, q], source[width + c, q]
            total = low + high
            part = share * total
            up = part + (high - part) * decay
            at = pl.ds((q % 2) * ROWS + q // 2, ROWS, stride=2 * ROWS)
            turned[0, at, :] = total - up
            turned[1, at, :] = up
        for y in range(size_y):
            for half in range(2):
                packed[half, pl.ds(c * size_y + y, count, stride=layer_rows), :] = swap_bits(
                    turned[half, pl.ds(y * ROWS, ROWS), :]
                )
        return carry

    lax.fori_loop(0, width, leave, 0)
    for half in range(2):
        for k in range(count):
            out[spread(k, last_bit, half)] = packed[half, pl.ds(k * layer_rows, layer_rows), :]


def run_block(mode, block, chunk, order, own, left, right, tables, other=None):
    smem = pl.BlockSpec(memory_space=pltpu.SMEM)
    vmem = pl.BlockSpec(memory_space=pltpu.VMEM)
    width, parts, rows, lanes = own.shape
    span = width + 2 * SUBSTEPS
    layer_rows = width * 2 * rows
    out = jax.ShapeDtypeStruct(own.shape, jnp.float32)
    scratch = [(span, parts, rows, lanes)] * 2
    if mode == "join":
        out = jax.ShapeDtypeStruct((2 * ROWS, layer_rows, lanes), jnp.float32)
        scratch = scratch + [(2, ROWS * layer_rows, lanes), (2, ROWS * 2 * rows, lanes)]
    extra = () if other is None else (other,)
    updates = own.size * 11
    return pl.pallas_call(
        partial(block_kernel, mode, block, chunk),
        out_shape=out,
        in_specs=[smem] + [vmem] * (3 + len(tables) + len(extra)),
        out_specs=vmem,
        scratch_shapes=[pltpu.VMEM(dims, jnp.float32) for dims in scratch],
        compiler_params=pltpu.CompilerParams(vmem_limit_bytes=32 * 1024 * 1024),
        cost_estimate=pl.CostEstimate(flops=updates * 14, bytes_accessed=own.size * 16, transcendentals=0),
        name=f"block{block}_{chunk}",
    )(order, own, left, right, *tables, *extra)


def local(density, levels, rate_index, on_rate, off_rate, gene_order):
    count, width, size_y, size_z = density.shape
    size = lax.axis_size("prot")
    onehot = rate_index[:, :, None] == jnp.arange(levels.shape[0], dtype=jnp.int32)[None, None, :]
    level_of = jnp.sum(jnp.where(onehot, levels[None, None, :], 0.0), axis=-1)
    rows = jnp.concatenate([level_of, jnp.zeros((count, ROWS - 3), jnp.float32)], axis=1)
    rows = jnp.broadcast_to(rows[:, :, None], (count, ROWS, size_z))
    both = jnp.concatenate([density.reshape(count, width * size_y, size_z), rows], axis=1)
    both = lax.all_to_all(both, "gene", 0, 0, tiled=True)
    low, high, *tables = enter((gene_order, on_rate, off_rate), both, width, size_y)
    parts = [low, high]
    forward = [(i, i + 1) for i in range(size - 1)]
    backward = [(i + 1, i) for i in range(size - 1)]
    for block in range(BLOCKS):
        sides = [(lax.ppermute(p, "prot", forward), lax.ppermute(p, "prot", backward)) for p in parts]
        if block < BLOCKS - 1:
            parts = [run_block("inside", block, c, gene_order, parts[c], *sides[c], tables) for c in range(2)]
        else:
            done = run_block("plain", block, 0, gene_order, parts[0], *sides[0], tables)
            done = run_block("join", block, 1, gene_order, parts[1], *sides[1], tables, done)
    done = lax.all_to_all(done, "gene", 0, 0, tiled=True)
    return done.reshape(density.shape)


def solution(mesh):
    in_specs = (P("gene", "prot", None, None), P(), P("gene", None), P(), P(), P())
    out_specs = P("gene", "prot", None, None)
    return jax.shard_map(local, mesh=mesh, in_specs=in_specs, out_specs=out_specs, check_vma=False)
```

time: 196 us -> 170 us (0.87)
  the two profiles are of different devices: /device:TPU:2 before, /device:TPU:4 now
where the time goes in v2:
time: 170 us; the launch traced here: 169 us
  starting transfers between devices  70.2 us (41%)
  blocking collectives  61.1 us (36%)
  Pallas kernels  27.7 us (16%)
  waiting for transfers between devices  6.54 us (4%)
  other arithmetic  1.98 us (1%)
    ppermute x8, starting transfers between devices, local(): lax.ppermute(p, 'prot', backward)  50.7 us
    all_to_all x1, blocking collectives, local(): both = lax.all_to_all(both, 'gene', 0, 0, tiled=True)  33.4 us
    all_to_all x1, blocking collectives, local(): done = lax.all_to_all(done, 'gene', 0, 0, tiled=True)  27.6 us
    pallas_call x8, Pallas kernels, run_block(): pl.pallas_call(partial(block_kernel, mode, block, chunk), out_shape=out,...  24.6 us
    ppermute x8, starting transfers between devices, local(): lax.ppermute(p, 'prot', forward)  19.5 us
    ppermute x8, waiting for transfers between devices, local(): lax.ppermute(p, 'prot', forward)  4.9 us
  transfers between devices with their start and end apart: 16, of which 3 were waited for; matrix products, arithmetic and copies ran while one was open for 0% of the time, Pallas kernels for 11%

profile of v2, /device:TPU:4, one launch (start us, length us, event | category | flops | bytes accessed | tf_op | source)
XLA Modules:
  0.0 168.9 jit_solution(493088385697958101)
XLA Ops:
  0.0 0.8 select_reduce_fusion
  1.0 1.2 pad_maximum_fusion
  2.2 33.4 %all_to_all.10.both = f32[16,104,128]{2,1,0:T(8,128)S(1)} all-to-all(f32[16,104,128]{2,1,0:T(8,128)S(1)} %pad_maximum_fusion), channel_id=1, replica_groups=mesh['gene'=16,'prot'=32] {'gene'}, dimensions={0} | all-to-all | bytes 1703936 | tf_op jit(solution)/shard_map/all_to_all | solution.py:242
  35.7 3.0 %enter.1 = (f32[6,16,8,128]{3,2,1,0:T(8,128)S(1)}, f32[6,16,8,128]{3,2,1,0:T(8,128)S(1)}, f32[2,2,18,8,128]{4,3,2,1,0:T(8,128)S(1)}, f32[2,4,8,128]{3,2,1,0:T(8,...) custom-call(s32[4]{0:T(128)S(1)} %copy-done, f32[8]{0:T(128)S(1)} %copy-done.1, ...), custom_call_target="tpu_custom_call" | custom-call | tf_op jit(solution)/shard_map/enter/pallas_call | solution.py:112
  38.7 1.9 %collective-permute-start.8 = (f32[6,16,8,128]{3,2,1,0:T(8,128)S(1)}, f32[6,16,8,128]{3,2,1,0:T(8,128)S(1)}, u32[]{:S(2)}, u32[]{:S(2)}) collective-permute-start(f32[6,16,8,128]{3,2,1,0:T(8,128)S(1)} %get-tuple-element.16.own), channel_id=1, source_target_pairs={{0,1},{1,2},{2,3},{3,4},{4,5},{5,6},{6,7},{7,8},{8,9},{9,10},{10,1... | collective-permute-start | bytes 1179656 | tf_op jit(solution)/shard_map/ppermute | solution.py:248
  40.6 7.9 %collective-permute-start.9 = (f32[6,16,8,128]{3,2,1,0:T(8,128)S(1)}, f32[6,16,8,128]{3,2,1,0:T(8,128)S(1)}, u32[]{:S(2)}, u32[]{:S(2)}) collective-permute-start(f32[6,16,8,128]{3,2,1,0:T(8,128)S(1)} %get-tuple-element.16.own), channel_id=1, source_target_pairs={{1,0},{2,1},{3,2},{4,3},{5,4},{6,5},{7,6},{8,7},{9,8},{10,9},{11,1... | collective-permute-start | bytes 1179656 | tf_op jit(solution)/shard_map/ppermute | solution.py:248
  48.5 1.9 %collective-permute-start = (f32[6,16,8,128]{3,2,1,0:T(8,128)S(1)}, f32[6,16,8,128]{3,2,1,0:T(8,128)S(1)}, u32[]{:S(2)}, u32[]{:S(2)}) collective-permute-start(f32[6,16,8,128]{3,2,1,0:T(8,128)S(1)} %get-tuple-element.11.own), channel_id=1, source_target_pairs={{0,1},{1,2},{2,3},{3,4},{4,5},{5,6},{6,7},{7,8},{8,9},{9,10},{10,1... | collective-permute-start | bytes 1179656 | tf_op jit(solution)/shard_map/ppermute | solution.py:248
  50.5 6.7 %collective-permute-start.1 = (f32[6,16,8,128]{3,2,1,0:T(8,128)S(1)}, f32[6,16,8,128]{3,2,1,0:T(8,128)S(1)}, u32[]{:S(2)}, u32[]{:S(2)}) collective-permute-start(f32[6,16,8,128]{3,2,1,0:T(8,128)S(1)} %get-tuple-element.11.own), channel_id=1, source_target_pairs={{1,0},{2,1},{3,2},{4,3},{5,4},{6,5},{7,6},{8,7},{9,8},{10,9},{11,1... | collective-permute-start | bytes 1179656 | tf_op jit(solution)/shard_map/ppermute | solution.py:248
  57.8 2.8 %block0_0.1.own = f32[6,16,8,128]{3,2,1,0:T(8,128)S(1)} custom-call(s32[4]{0:T(128)S(1)} %copy-done, f32[6,16,8,128]{3,2,1,0:T(8,128)S(1)} %get-tuple-element.16.own, f32[6,16,8,128]{3,2,1,0:T(8,128)S(1)} %collective-permute-done.8.left, f32[6,16,8,128]{3,2,1,0:T(8,128)S(1)} %collective-permute-done.9.right, ...), custom_call_target="tpu_custom_call" | custom-call | flops 15138816 | bytes 1572864 | tf_op jit(solution)/shard_map/block0_0/pallas_call | solution.py:222
  60.6 5.9 %collective-permute-start.10 = (f32[6,16,8,128]{3,2,1,0:T(8,128)S(1)}, f32[6,16,8,128]{3,2,1,0:T(8,128)S(1)}, u32[]{:S(2)}, u32[]{:S(2)}) collective-permute-start(f32[6,16,8,128]{3,2,1,0:T(8,128)S(1)} %block0_0.1.own), channel_id=1, source_target_pairs={{0,1},{1,2},{2,3},{3,4},{4,5},{5,6},{6,7},{7,8},{8,9},{9,10},{10,1... | collective-permute-start | bytes 1179656 | tf_op jit(solution)/shard_map/ppermute | solution.py:248
  66.5 2.9 %collective-permute-start.11 = (f32[6,16,8,128]{3,2,1,0:T(8,128)S(1)}, f32[6,16,8,128]{3,2,1,0:T(8,128)S(1)}, u32[]{:S(2)}, u32[]{:S(2)}) collective-permute-start(f32[6,16,8,128]{3,2,1,0:T(8,128)S(1)} %block0_0.1.own), channel_id=1, source_target_pairs={{1,0},{2,1},{3,2},{4,3},{5,4},{6,5},{7,6},{8,7},{9,8},{10,9},{11,1... | collective-permute-start | bytes 1179656 | tf_op jit(solution)/shard_map/ppermute | solution.py:248
  69.5 2.8 %block0_1.1.own = f32[6,16,8,128]{3,2,1,0:T(8,128)S(1)} custom-call(s32[4]{0:T(128)S(1)} %copy-done, f32[6,16,8,128]{3,2,1,0:T(8,128)S(1)} %get-tuple-element.11.own, f32[6,16,8,128]{3,2,1,0:T(8,128)S(1)} %collective-permute-done.left, f32[6,16,8,128]{3,2,1,0:T(8,128)S(1)} %collective-permute-done.1.right, ...), custom_call_target="tpu_custom_call" | custom-call | flops 15138816 | bytes 1572864 | tf_op jit(solution)/shard_map/block0_1/pallas_call | solution.py:222
  72.3 1.9 %collective-permute-start.2 = (f32[6,16,8,128]{3,2,1,0:T(8,128)S(1)}, f32[6,16,8,128]{3,2,1,0:T(8,128)S(1)}, u32[]{:S(2)}, u32[]{:S(2)}) collective-permute-start(f32[6,16,8,128]{3,2,1,0:T(8,128)S(1)} %block0_1.1.own), channel_id=1, source_target_pairs={{0,1},{1,2},{2,3},{3,4},{4,5},{5,6},{6,7},{7,8},{8,9},{9,10},{10,1... | collective-permute-start | bytes 1179656 | tf_op jit(solution)/shard_map/ppermute | solution.py:248
  74.2 6.7 %collective-permute-start.3 = (f32[6,16,8,128]{3,2,1,0:T(8,128)S(1)}, f32[6,16,8,128]{3,2,1,0:T(8,128)S(1)}, u32[]{:S(2)}, u32[]{:S(2)}) collective-permute-start(f32[6,16,8,128]{3,2,1,0:T(8,128)S(1)} %block0_1.1.own), channel_id=1, source_target_pairs={{1,0},{2,1},{3,2},{4,3},{5,4},{6,5},{7,6},{8,7},{9,8},{10,9},{11,1... | collective-permute-start | bytes 1179656 | tf_op jit(solution)/shard_map/ppermute | solution.py:248
  80.9 2.8 %block1_0.1.own = f32[6,16,8,128]{3,2,1,0:T(8,128)S(1)} custom-call(s32[4]{0:T(128)S(1)} %copy-done, f32[6,16,8,128]{3,2,1,0:T(8,128)S(1)} %block0_0.1.own, f32[6,16,8,128]{3,2,1,0:T(8,128)S(1)} %collective-permute-done.10.left, f32[6,16,8,128]{3,2,1,0:T(8,128)S(1)} %collective-permute-done.11.right, f32[2,2,18,8,128]{4,3,2,1,0:T(8,128)S(1)} %get-tuple-element.12.x_table, ...), custom_call_target="tpu_custom_call" | custom-call | flops 15138816 | bytes 1572864 | tf_op jit(solution)/shard_map/block1_0/pallas_call | solution.py:222
  83.7 2.1 %collective-permute-start.12 = (f32[6,16,8,128]{3,2,1,0:T(8,128)S(1)}, f32[6,16,8,128]{3,2,1,0:T(8,128)S(1)}, u32[]{:S(2)}, u32[]{:S(2)}) collective-permute-start(f32[6,16,8,128]{3,2,1,0:T(8,128)S(1)} %block1_0.1.own), channel_id=1, source_target_pairs={{0,1},{1,2},{2,3},{3,4},{4,5},{5,6},{6,7},{7,8},{8,9},{9,10},{10,1... | collective-permute-start | bytes 1179656 | tf_op jit(solution)/shard_map/ppermute | solution.py:248
  85.8 6.5 %collective-permute-start.13 = (f32[6,16,8,128]{3,2,1,0:T(8,128)S(1)}, f32[6,16,8,128]{3,2,1,0:T(8,128)S(1)}, u32[]{:S(2)}, u32[]{:S(2)}) collective-permute-start(f32[6,16,8,128]{3,2,1,0:T(8,128)S(1)} %block1_0.1.own), channel_id=1, source_target_pairs={{1,0},{2,1},{3,2},{4,3},{5,4},{6,5},{7,6},{8,7},{9,8},{10,9},{11,1... | collective-permute-start | bytes 1179656 | tf_op jit(solution)/shard_map/ppermute | solution.py:248
  92.3 2.8 %block1_1.1.own = f32[6,16,8,128]{3,2,1,0:T(8,128)S(1)} custom-call(s32[4]{0:T(128)S(1)} %copy-done, f32[6,16,8,128]{3,2,1,0:T(8,128)S(1)} %block0_1.1.own, f32[6,16,8,128]{3,2,1,0:T(8,128)S(1)} %collective-permute-done.2.left, f32[6,16,8,128]{3,2,1,0:T(8,128)S(1)} %collective-permute-done.3.right, f32[2,2,18,8,128]{4,3,2,1,0:T(8,128)S(1)} %get-tuple-element.12.x_table, ...), custom_call_target="tpu_custom_call" | custom-call | flops 15138816 | bytes 1572864 | tf_op jit(solution)/shard_map/block1_1/pallas_call | solution.py:222
  95.1 1.9 %collective-permute-start.4 = (f32[6,16,8,128]{3,2,1,0:T(8,128)S(1)}, f32[6,16,8,128]{3,2,1,0:T(8,128)S(1)}, u32[]{:S(2)}, u32[]{:S(2)}) collective-permute-start(f32[6,16,8,128]{3,2,1,0:T(8,128)S(1)} %block1_1.1.own), channel_id=1, source_target_pairs={{0,1},{1,2},{2,3},{3,4},{4,5},{5,6},{6,7},{7,8},{8,9},{9,10},{10,1... | collective-permute-start | bytes 1179656 | tf_op jit(solution)/shard_map/ppermute | solution.py:248
  97.0 6.8 %collective-permute-start.5 = (f32[6,16,8,128]{3,2,1,0:T(8,128)S(1)}, f32[6,16,8,128]{3,2,1,0:T(8,128)S(1)}, u32[]{:S(2)}, u32[]{:S(2)}) collective-permute-start(f32[6,16,8,128]{3,2,1,0:T(8,128)S(1)} %block1_1.1.own), channel_id=1, source_target_pairs={{1,0},{2,1},{3,2},{4,3},{5,4},{6,5},{7,6},{8,7},{9,8},{10,9},{11,1... | collective-permute-start | bytes 1179656 | tf_op jit(solution)/shard_map/ppermute | solution.py:248
  103.9 2.8 %block2_0.1.own = f32[6,16,8,128]{3,2,1,0:T(8,128)S(1)} custom-call(s32[4]{0:T(128)S(1)} %copy-done, f32[6,16,8,128]{3,2,1,0:T(8,128)S(1)} %block1_0.1.own, f32[6,16,8,128]{3,2,1,0:T(8,128)S(1)} %collective-permute-done.12.left, f32[6,16,8,128]{3,2,1,0:T(8,128)S(1)} %collective-permute-done.13.right, f32[2,2,18,8,128]{4,3,2,1,0:T(8,128)S(1)} %get-tuple-element.12.x_table, ...), custom_call_target="tpu_custom_call" | custom-call | flops 15138816 | bytes 1572864 | tf_op jit(solution)/shard_map/block2_0/pallas_call | solution.py:222
  106.7 1.9 %collective-permute-start.14 = (f32[6,16,8,128]{3,2,1,0:T(8,128)S(1)}, f32[6,16,8,128]{3,2,1,0:T(8,128)S(1)}, u32[]{:S(2)}, u32[]{:S(2)}) collective-permute-start(f32[6,16,8,128]{3,2,1,0:T(8,128)S(1)} %block2_0.1.own), channel_id=1, source_target_pairs={{0,1},{1,2},{2,3},{3,4},{4,5},{5,6},{6,7},{7,8},{8,9},{9,10},{10,1... | collective-permute-start | bytes 1179656 | tf_op jit(solution)/shard_map/ppermute | solution.py:248
  108.6 6.7 %collective-permute-start.15 = (f32[6,16,8,128]{3,2,1,0:T(8,128)S(1)}, f32[6,16,8,128]{3,2,1,0:T(8,128)S(1)}, u32[]{:S(2)}, u32[]{:S(2)}) collective-permute-start(f32[6,16,8,128]{3,2,1,0:T(8,128)S(1)} %block2_0.1.own), channel_id=1, source_target_pairs={{1,0},{2,1},{3,2},{4,3},{5,4},{6,5},{7,6},{8,7},{9,8},{10,9},{11,1... | collective-permute-start | bytes 1179656 | tf_op jit(solution)/shard_map/ppermute | solution.py:248
  115.3 2.8 %block2_1.1.own = f32[6,16,8,128]{3,2,1,0:T(8,128)S(1)} custom-call(s32[4]{0:T(128)S(1)} %copy-done, f32[6,16,8,128]{3,2,1,0:T(8,128)S(1)} %block1_1.1.own, f32[6,16,8,128]{3,2,1,0:T(8,128)S(1)} %collective-permute-done.4.left, f32[6,16,8,128]{3,2,1,0:T(8,128)S(1)} %collective-permute-done.5.right, f32[2,2,18,8,128]{4,3,2,1,0:T(8,128)S(1)} %get-tuple-element.12.x_table, ...), custom_call_target="tpu_custom_call" | custom-call | flops 15138816 | bytes 1572864 | tf_op jit(solution)/shard_map/block2_1/pallas_call | solution.py:222
  118.1 1.9 %collective-permute-start.6 = (f32[6,16,8,128]{3,2,1,0:T(8,128)S(1)}, f32[6,16,8,128]{3,2,1,0:T(8,128)S(1)}, u32[]{:S(2)}, u32[]{:S(2)}) collective-permute-start(f32[6,16,8,128]{3,2,1,0:T(8,128)S(1)} %block2_1.1.own), channel_id=1, source_target_pairs={{0,1},{1,2},{2,3},{3,4},{4,5},{5,6},{6,7},{7,8},{8,9},{9,10},{10,1... | collective-permute-start | bytes 1179656 | tf_op jit(solution)/shard_map/ppermute | solution.py:248
  120.0 6.7 %collective-permute-start.7 = (f32[6,16,8,128]{3,2,1,0:T(8,128)S(1)}, f32[6,16,8,128]{3,2,1,0:T(8,128)S(1)}, u32[]{:S(2)}, u32[]{:S(2)}) collective-permute-start(f32[6,16,8,128]{3,2,1,0:T(8,128)S(1)} %block2_1.1.own), channel_id=1, source_target_pairs={{1,0},{2,1},{3,2},{4,3},{5,4},{6,5},{7,6},{8,7},{9,8},{10,9},{11,1... | collective-permute-start | bytes 1179656 | tf_op jit(solution)/shard_map/ppermute | solution.py:248
  126.7 2.6 %block3_0.1.rest_0_ = f32[6,16,8,128]{3,2,1,0:T(8,128)S(1)} custom-call(s32[4]{0:T(128)S(1)} %copy-done, f32[6,16,8,128]{3,2,1,0:T(8,128)S(1)} %block2_0.1.own, f32[6,16,8,128]{3,2,1,0:T(8,128)S(1)} %collective-permute-done.14.left, f32[6,16,8,128]{3,2,1,0:T(8,128)S(1)} %collective-permute-done.15.right, ...), custom_call_target="tpu_custom_call" | custom-call | flops 15138816 | bytes 1572864 | tf_op jit(solution)/shard_map/block3_0/pallas_call | solution.py:222
  129.3 4.9 %collective-permute-done.6.left = f32[6,16,8,128]{3,2,1,0:T(8,128)S(1)} collective-permute-done((f32[6,16,8,128]{3,2,1,0:T(8,128)S(1)}, f32[6,16,8,128]{3,2,1,0:T(8,128)S(1)}, u32[]{:S(2)}, u32[]{:S(2)}) %collective-permute-start.6) | collective-permute-done | bytes 393248 | tf_op jit(solution)/shard_map/ppermute | solution.py:248
  134.2 0.9 collective-permute-done.7.right
  135.1 5.2 %block3_1.1 = f32[16,96,128]{2,1,0:T(8,128)S(1)} custom-call(s32[4]{0:T(128)S(1)} %copy-done, f32[6,16,8,128]{3,2,1,0:T(8,128)S(1)} %block2_1.1.own, f32[6,16,8,128]{3,2,1,0:T(8,128)S(1)} %collective-permute-done.6.left, f32[6,16,8,128]{3,2,1,0:T(8,128)S(1)} %collective-permute-done.7.right, f32[2,2,18,8,128]{4,3,2,1,0:T(8,128)S(1)} %get-tuple-element.12.x_table, ...), custom_call_target="tpu_custom_call" | custom-call | flops 15138816 | bytes 1572864 | tf_op jit(solution)/shard_map/block3_1/pallas_call | solution.py:222
  140.3 27.6 %all_to_all.11 = f32[16,96,128]{2,1,0:T(8,128)S(1)} all-to-all(f32[16,96,128]{2,1,0:T(8,128)S(1)} %block3_1.1), channel_id=1, replica_groups=mesh['gene'=16,'prot'=32] {'gene'}, dimensions={0} | all-to-all | bytes 1572864 | tf_op jit(solution)/shard_map/all_to_all | solution.py:254
  168.0 0.9 copy.11
  (23 shorter events, 0.9 us)
Async XLA Ops:
  2.2 33.5 %copy-start = (s32[4]{0:T(128)S(1)}, s32[4]{0:T(128)}, u32[]{:S(2)}) copy-start(s32[4]{0:T(128)} %order.17) | copy-start | bytes 52
  2.2 33.5 %copy-start.1 = (f32[8]{0:T(128)S(1)}, f32[8]{0:T(128)}, u32[]{:S(2)}) copy-start(f32[8]{0:T(128)} %on_rate.1) | copy-start | bytes 100
  2.2 33.5 %copy-start.2 = (f32[8]{0:T(128)S(1)}, f32[8]{0:T(128)}, u32[]{:S(2)}) copy-start(f32[8]{0:T(128)} %off_rate.1) | copy-start | bytes 100
  38.7 18.4 %collective-permute-start.8 = (f32[6,16,8,128]{3,2,1,0:T(8,128)S(1)}, f32[6,16,8,128]{3,2,1,0:T(8,128)S(1)}, u32[]{:S(2)}, u32[]{:S(2)}) collective-permute-start(f32[6,16,8,128]{3,2,1,0:T(8,128)S(1)} %get-tuple-element.16.own), channel_id=1, source_target_pairs={{0,1},{1,2},{2,3},{3,4},{4,5},{5,6},{6,7},{7,8},{8,9},{9,10},{10,1... | collective-permute-start | bytes 1179656 | tf_op jit(solution)/shard_map/ppermute | solution.py:248
  40.6 17.2 %collective-permute-start.9 = (f32[6,16,8,128]{3,2,1,0:T(8,128)S(1)}, f32[6,16,8,128]{3,2,1,0:T(8,128)S(1)}, u32[]{:S(2)}, u32[]{:S(2)}) collective-permute-start(f32[6,16,8,128]{3,2,1,0:T(8,128)S(1)} %get-tuple-element.16.own), channel_id=1, source_target_pairs={{1,0},{2,1},{3,2},{4,3},{5,4},{6,5},{7,6},{8,7},{9,8},{10,9},{11,1... | collective-permute-start | bytes 1179656 | tf_op jit(solution)/shard_map/ppermute | solution.py:248
  48.5 20.9 %collective-permute-start = (f32[6,16,8,128]{3,2,1,0:T(8,128)S(1)}, f32[6,16,8,128]{3,2,1,0:T(8,128)S(1)}, u32[]{:S(2)}, u32[]{:S(2)}) collective-permute-start(f32[6,16,8,128]{3,2,1,0:T(8,128)S(1)} %get-tuple-element.11.own), channel_id=1, source_target_pairs={{0,1},{1,2},{2,3},{3,4},{4,5},{5,6},{6,7},{7,8},{8,9},{9,10},{10,1... | collective-permute-start | bytes 1179656 | tf_op jit(solution)/shard_map/ppermute | solution.py:248
  50.5 19.0 %collective-permute-start.1 = (f32[6,16,8,128]{3,2,1,0:T(8,128)S(1)}, f32[6,16,8,128]{3,2,1,0:T(8,128)S(1)}, u32[]{:S(2)}, u32[]{:S(2)}) collective-permute-start(f32[6,16,8,128]{3,2,1,0:T(8,128)S(1)} %get-tuple-element.11.own), channel_id=1, source_target_pairs={{1,0},{2,1},{3,2},{4,3},{5,4},{6,5},{7,6},{8,7},{9,8},{10,9},{11,1... | collective-permute-start | bytes 1179656 | tf_op jit(solution)/shard_map/ppermute | solution.py:248
  60.6 20.2 %collective-permute-start.10 = (f32[6,16,8,128]{3,2,1,0:T(8,128)S(1)}, f32[6,16,8,128]{3,2,1,0:T(8,128)S(1)}, u32[]{:S(2)}, u32[]{:S(2)}) collective-permute-start(f32[6,16,8,128]{3,2,1,0:T(8,128)S(1)} %block0_0.1.own), channel_id=1, source_target_pairs={{0,1},{1,2},{2,3},{3,4},{4,5},{5,6},{6,7},{7,8},{8,9},{9,10},{10,1... | collective-permute-start | bytes 1179656 | tf_op jit(solution)/shard_map/ppermute | solution.py:248
  66.5 14.3 %collective-permute-start.11 = (f32[6,16,8,128]{3,2,1,0:T(8,128)S(1)}, f32[6,16,8,128]{3,2,1,0:T(8,128)S(1)}, u32[]{:S(2)}, u32[]{:S(2)}) collective-permute-start(f32[6,16,8,128]{3,2,1,0:T(8,128)S(1)} %block0_0.1.own), channel_id=1, source_target_pairs={{1,0},{2,1},{3,2},{4,3},{5,4},{6,5},{7,6},{8,7},{9,8},{10,9},{11,1... | collective-permute-start | bytes 1179656 | tf_op jit(solution)/shard_map/ppermute | solution.py:248
  72.3 20.0 %collective-permute-start.2 = (f32[6,16,8,128]{3,2,1,0:T(8,128)S(1)}, f32[6,16,8,128]{3,2,1,0:T(8,128)S(1)}, u32[]{:S(2)}, u32[]{:S(2)}) collective-permute-start(f32[6,16,8,128]{3,2,1,0:T(8,128)S(1)} %block0_1.1.own), channel_id=1, source_target_pairs={{0,1},{1,2},{2,3},{3,4},{4,5},{5,6},{6,7},{7,8},{8,9},{9,10},{10,1... | collective-permute-start | bytes 1179656 | tf_op jit(solution)/shard_map/ppermute | solution.py:248
  74.2 18.1 %collective-permute-start.3 = (f32[6,16,8,128]{3,2,1,0:T(8,128)S(1)}, f32[6,16,8,128]{3,2,1,0:T(8,128)S(1)}, u32[]{:S(2)}, u32[]{:S(2)}) collective-permute-start(f32[6,16,8,128]{3,2,1,0:T(8,128)S(1)} %block0_1.1.own), channel_id=1, source_target_pairs={{1,0},{2,1},{3,2},{4,3},{5,4},{6,5},{7,6},{8,7},{9,8},{10,9},{11,1... | collective-permute-start | bytes 1179656 | tf_op jit(solution)/shard_map/ppermute | solution.py:248
  83.7 20.2 %collective-permute-start.12 = (f32[6,16,8,128]{3,2,1,0:T(8,128)S(1)}, f32[6,16,8,128]{3,2,1,0:T(8,128)S(1)}, u32[]{:S(2)}, u32[]{:S(2)}) collective-permute-start(f32[6,16,8,128]{3,2,1,0:T(8,128)S(1)} %block1_0.1.own), channel_id=1, source_target_pairs={{0,1},{1,2},{2,3},{3,4},{4,5},{5,6},{6,7},{7,8},{8,9},{9,10},{10,1... | collective-permute-start | bytes 1179656 | tf_op jit(solution)/shard_map/ppermute | solution.py:248
  85.8 18.1 %collective-permute-start.13 = (f32[6,16,8,128]{3,2,1,0:T(8,128)S(1)}, f32[6,16,8,128]{3,2,1,0:T(8,128)S(1)}, u32[]{:S(2)}, u32[]{:S(2)}) collective-permute-start(f32[6,16,8,128]{3,2,1,0:T(8,128)S(1)} %block1_0.1.own), channel_id=1, source_target_pairs={{1,0},{2,1},{3,2},{4,3},{5,4},{6,5},{7,6},{8,7},{9,8},{10,9},{11,1... | collective-permute-start | bytes 1179656 | tf_op jit(solution)/shard_map/ppermute | solution.py:248
  95.1 20.2 %collective-permute-start.4 = (f32[6,16,8,128]{3,2,1,0:T(8,128)S(1)}, f32[6,16,8,128]{3,2,1,0:T(8,128)S(1)}, u32[]{:S(2)}, u32[]{:S(2)}) collective-permute-start(f32[6,16,8,128]{3,2,1,0:T(8,128)S(1)} %block1_1.1.own), channel_id=1, source_target_pairs={{0,1},{1,2},{2,3},{3,4},{4,5},{5,6},{6,7},{7,8},{8,9},{9,10},{10,1... | collective-permute-start | bytes 1179656 | tf_op jit(solution)/shard_map/ppermute | solution.py:248
  97.0 18.3 %collective-permute-start.5 = (f32[6,16,8,128]{3,2,1,0:T(8,128)S(1)}, f32[6,16,8,128]{3,2,1,0:T(8,128)S(1)}, u32[]{:S(2)}, u32[]{:S(2)}) collective-permute-start(f32[6,16,8,128]{3,2,1,0:T(8,128)S(1)} %block1_1.1.own), channel_id=1, source_target_pairs={{1,0},{2,1},{3,2},{4,3},{5,4},{6,5},{7,6},{8,7},{9,8},{10,9},{11,1... | collective-permute-start | bytes 1179656 | tf_op jit(solution)/shard_map/ppermute | solution.py:248
  106.7 20.0 %collective-permute-start.14 = (f32[6,16,8,128]{3,2,1,0:T(8,128)S(1)}, f32[6,16,8,128]{3,2,1,0:T(8,128)S(1)}, u32[]{:S(2)}, u32[]{:S(2)}) collective-permute-start(f32[6,16,8,128]{3,2,1,0:T(8,128)S(1)} %block2_0.1.own), channel_id=1, source_target_pairs={{0,1},{1,2},{2,3},{3,4},{4,5},{5,6},{6,7},{7,8},{8,9},{9,10},{10,1... | collective-permute-start | bytes 1179656 | tf_op jit(solution)/shard_map/ppermute | solution.py:248
  108.6 18.1 %collective-permute-start.15 = (f32[6,16,8,128]{3,2,1,0:T(8,128)S(1)}, f32[6,16,8,128]{3,2,1,0:T(8,128)S(1)}, u32[]{:S(2)}, u32[]{:S(2)}) collective-permute-start(f32[6,16,8,128]{3,2,1,0:T(8,128)S(1)} %block2_0.1.own), channel_id=1, source_target_pairs={{1,0},{2,1},{3,2},{4,3},{5,4},{6,5},{7,6},{8,7},{9,8},{10,9},{11,1... | collective-permute-start | bytes 1179656 | tf_op jit(solution)/shard_map/ppermute | solution.py:248
  118.1 16.1 %collective-permute-start.6 = (f32[6,16,8,128]{3,2,1,0:T(8,128)S(1)}, f32[6,16,8,128]{3,2,1,0:T(8,128)S(1)}, u32[]{:S(2)}, u32[]{:S(2)}) collective-permute-start(f32[6,16,8,128]{3,2,1,0:T(8,128)S(1)} %block2_1.1.own), channel_id=1, source_target_pairs={{0,1},{1,2},{2,3},{3,4},{4,5},{5,6},{6,7},{7,8},{8,9},{9,10},{10,1... | collective-permute-start | bytes 1179656 | tf_op jit(solution)/shard_map/ppermute | solution.py:248
  120.0 15.1 %collective-permute-start.7 = (f32[6,16,8,128]{3,2,1,0:T(8,128)S(1)}, f32[6,16,8,128]{3,2,1,0:T(8,128)S(1)}, u32[]{:S(2)}, u32[]{:S(2)}) collective-permute-start(f32[6,16,8,128]{3,2,1,0:T(8,128)S(1)} %block2_1.1.own), channel_id=1, source_target_pairs={{1,0},{2,1},{3,2},{4,3},{5,4},{6,5},{7,6},{8,7},{9,8},{10,9},{11,1... | collective-permute-start | bytes 1179656 | tf_op jit(solution)/shard_map/ppermute | solution.py:248

commit v3 on v2

--- a/solution.py
+++ b/solution.py
@@ -42,11 +42,45 @@
     return value
 
 
-def entry_kernel(width, size_y, order, on_rate, off_rate, both, low, high, x_table, y_table, z_table, mix_table, packed, turned):
+def entry_kernel(chunk, layer_rows, order, both, out, packed, turned):
     last_bit = BLOCKS - 1 - order[BLOCKS - 1]
-    layer_rows = width * size_y
+    size_y = turned.shape[0] // ROWS
+    count = both.shape[0] // 2
+    for k in range(count):
+        packed[pl.ds(k * layer_rows, layer_rows), :] = both[spread(k, last_bit, chunk), 0:layer_rows, :]
+
+    def layer(x, carry):
+        for y in range(size_y):
+            turned[pl.ds(y * ROWS, ROWS), :] = swap_bits(packed[pl.ds(x * size_y + y, count, stride=layer_rows), :])
+        for q in range(2 * ROWS):
+            out[x, q] = turned[pl.ds((q % 2) * ROWS + q // 2, ROWS, stride=2 * ROWS), :]
+        return carry
+
+    lax.fori_loop(0, layer_rows // size_y, layer, 0)
+
+
+def enter(chunk, order, both, width, size_y):
+    lanes = both.shape[2]
+    vmem = pl.BlockSpec(memory_space=pltpu.VMEM)
+    return pl.pallas_call(
+        partial(entry_kernel, chunk, width * size_y),
+        out_shape=jax.ShapeDtypeStruct((width, 2 * ROWS, ROWS, lanes), jnp.float32),
+        in_specs=[pl.BlockSpec(memory_space=pltpu.SMEM), vmem],
+        out_specs=vmem,
+        scratch_shapes=[
+            pltpu.VMEM((ROWS * width * size_y, lanes), jnp.float32),
+            pltpu.VMEM((size_y * ROWS, lanes), jnp.float32),
+        ],
+        compiler_params=pltpu.CompilerParams(vmem_limit_bytes=32 * 1024 * 1024),
+        name=f"enter{chunk}",
+    )(order, both)
+
+
+def tables_kernel(width, size_y, order, on_rate, off_rate, levels, both, x_table, y_table, z_table, mix_table):
+    last_bit = BLOCKS - 1 - order[BLOCKS - 1]
     size_z = both.shape[2]
     count = both.shape[0] // 2
+    layer_rows = width * size_y
     shape = (ROWS, size_z)
     place = lax.axis_index("prot")
     total_x = width * lax.axis_size("prot")
@@ -55,28 +89,15 @@
     col = lax.broadcasted_iota(jnp.int32, shape, 1)
     lane_state = jnp.bitwise_and(lax.broadcasted_iota(jnp.int32, (1, size_z), 1), count - 1)
     for chunk in range(2):
-        for k in range(count):
-            packed[chunk, pl.ds(k * layer_rows, layer_rows), :] = both[spread(k, last_bit, chunk), 0:layer_rows, :]
-
-    def layer(x, carry):
-        for chunk in range(2):
-            for y in range(size_y):
-                turned[chunk, pl.ds(y * ROWS, ROWS), :] = swap_bits(
-                    packed[chunk, pl.ds(x * size_y + y, count, stride=layer_rows), :]
-                )
-        for chunk, out in enumerate((low, high)):
-            for q in range(2 * ROWS):
-                out[x, q] = turned[chunk, pl.ds((q % 2) * ROWS + q // 2, ROWS, stride=2 * ROWS), :]
-        return carry
-
-    lax.fori_loop(0, width, layer, 0)
-    for chunk in range(2):
         lines = []
         for r in range(3):
             line = jnp.zeros((1, size_z), jnp.float32)
             for k in range(count):
                 line = jnp.where(lane_state == k, both[spread(k, last_bit, chunk), layer_rows + r : layer_rows + r + 1, :], line)
-            lines.append(jnp.broadcast_to(line, shape))
+            level = jnp.zeros((1, size_z), jnp.float32)
+            for m in range(levels.shape[0]):
+                level = jnp.where(line == float(m), levels[m], level)
+            lines.append(jnp.broadcast_to(level, shape))
         lx, ly, lz = lines
         for c in range(x_table.shape[2]):
             cell = first_x - SUBSTEPS + c
@@ -102,24 +123,18 @@
             mix_table[block, 1, c] = decay
 
 
-def enter(scalars, both, width, size_y):
-    lanes = both.shape[2]
+def make_tables(scalars, both, width, size_y):
     smem = pl.BlockSpec(memory_space=pltpu.SMEM)
     vmem = pl.BlockSpec(memory_space=pltpu.VMEM)
-    tile = (ROWS, lanes)
-    chunk = (width, 2 * ROWS) + tile
-    dims = [chunk, chunk, (2, 2, width + 2 * SUBSTEPS) + tile, (2, 4) + tile, (2, 2, ROWS) + tile, (BLOCKS, 2, width) + tile]
+    tile = (ROWS, both.shape[2])
+    dims = [(2, 2, width + 2 * SUBSTEPS) + tile, (2, 4) + tile, (2, 2, ROWS) + tile, (BLOCKS, 2, width) + tile]
     return pl.pallas_call(
-        partial(entry_kernel, width, size_y),
+        partial(tables_kernel, width, size_y),
         out_shape=tuple(jax.ShapeDtypeStruct(d, jnp.float32) for d in dims),
-        in_specs=[smem] * 3 + [vmem],
+        in_specs=[smem] * len(scalars) + [vmem],
         out_specs=(vmem,) * len(dims),
-        scratch_shapes=[
-            pltpu.VMEM((2, ROWS * width * size_y, lanes), jnp.float32),
-            pltpu.VMEM((2, size_y * ROWS, lanes), jnp.float32),
-        ],
         compiler_params=pltpu.CompilerParams(vmem_limit_bytes=32 * 1024 * 1024),
-        name="enter",
+        name="tables",
     )(*scalars, both)
 
 
@@ -140,8 +155,6 @@
     apart = jnp.left_shift(1, inner_bit)
 
     def finish(c, q, value):
-        if mode != "inside":
-            return value
         mate = jnp.where(is_high, pltpu.roll(value, apart, 1), pltpu.roll(value, lanes - apart, 1))
         total = value + mate
         part = mix_table[block, 0, c] * total
@@ -172,38 +185,37 @@
                 z_part = z_table[chunk, 0, j] * z_up + z_table[chunk, 1, j] * z_down
                 fresh.append(sums[q] + (y_part + z_part))
             for q in range(parts):
-                if final and mode != "join":
+                if final and mode == "inside":
                     out[c - width, q] = finish(c - width, q, fresh[q])
                 else:
                     target[c, q] = fresh[q]
         read = lambda c, q, ref=target: ref[c, q]
-    if mode != "join":
+    if mode == "inside":
         return
     source = target
-    packed, turned = rest[3:]
+    packed, turned = (out, rest[3]) if mode == "plain" else rest[3:]
     layer_rows = width * size_y
 
     def leave(c, carry):
+        for q in range(parts):
+            turned[pl.ds((q % 2) * ROWS + q // 2, ROWS, stride=2 * ROWS), :] = source[width + c, q]
+        for y in range(size_y):
+            packed[pl.ds(c * size_y + y, count, stride=layer_rows), :] = swap_bits(turned[pl.ds(y * ROWS, ROWS), :])
+        return carry
+
+    lax.fori_loop(0, width, leave, 0)
+    if mode == "plain":
+        return
+    for c in range(width):
         share, decay = mix_table[block, 0, c], mix_table[block, 1, c]
-        for q in range(parts):
-            low, high = other[c, q], source[width + c, q]
-            total = low + high
-            part = share * total
-            up = part + (high - part) * decay
-            at = pl.ds((q % 2) * ROWS + q // 2, ROWS, stride=2 * ROWS)
-            turned[0, at, :] = total - up
-            turned[1, at, :] = up
-        for y in range(size_y):
-            for half in range(2):
-                packed[half, pl.ds(c * size_y + y, count, stride=layer_rows), :] = swap_bits(
-                    turned[half, pl.ds(y * ROWS, ROWS), :]
-                )
-        return carry
-
-    lax.fori_loop(0, width, leave, 0)
-    for half in range(2):
         for k in range(count):
-            out[spread(k, last_bit, half)] = packed[half, pl.ds(k * layer_rows, layer_rows), :]
+            for r in range(c * size_y, (c + 1) * size_y, ROWS):
+                low, high = other[pl.ds(k * layer_rows + r, ROWS), :], packed[pl.ds(k * layer_rows + r, ROWS), :]
+                total = low + high
+                part = share * total
+                up = part + (high - part) * decay
+                out[spread(k, last_bit, 1), pl.ds(r, ROWS), :] = up
+                out[spread(k, last_bit, 0), pl.ds(r, ROWS), :] = total - up
 
 
 def run_block(mode, block, chunk, order, own, left, right, tables, other=None):
@@ -214,9 +226,12 @@
     layer_rows = width * 2 * rows
     out = jax.ShapeDtypeStruct(own.shape, jnp.float32)
     scratch = [(span, parts, rows, lanes)] * 2
+    if mode == "plain":
+        out = jax.ShapeDtypeStruct((ROWS * layer_rows, lanes), jnp.float32)
+        scratch = scratch + [(ROWS * 2 * rows, lanes)]
     if mode == "join":
         out = jax.ShapeDtypeStruct((2 * ROWS, layer_rows, lanes), jnp.float32)
-        scratch = scratch + [(2, ROWS * layer_rows, lanes), (2, ROWS * 2 * rows, lanes)]
+        scratch = scratch + [(ROWS * layer_rows, lanes), (ROWS * 2 * rows, lanes)]
     extra = () if other is None else (other,)
     updates = own.size * 11
     return pl.pallas_call(
@@ -234,14 +249,13 @@
 def local(density, levels, rate_index, on_rate, off_rate, gene_order):
     count, width, size_y, size_z = density.shape
     size = lax.axis_size("prot")
-    onehot = rate_index[:, :, None] == jnp.arange(levels.shape[0], dtype=jnp.int32)[None, None, :]
-    level_of = jnp.sum(jnp.where(onehot, levels[None, None, :], 0.0), axis=-1)
-    rows = jnp.concatenate([level_of, jnp.zeros((count, ROWS - 3), jnp.float32)], axis=1)
+    rows = jnp.pad(rate_index.astype(jnp.float32), ((0, 0), (0, ROWS - rate_index.shape[1])))
     rows = jnp.broadcast_to(rows[:, :, None], (count, ROWS, size_z))
     both = jnp.concatenate([density.reshape(count, width * size_y, size_z), rows], axis=1)
     both = lax.all_to_all(both, "gene", 0, 0, tiled=True)
-    low, high, *tables = enter((gene_order, on_rate, off_rate), both, width, size_y)
-    parts = [low, high]
+    parts = [enter(chunk, gene_order, both, width, size_y) for chunk in range(2)]
+    levels, parts[1] = lax.optimization_barrier((levels, parts[1]))
+    tables = make_tables((gene_order, on_rate, off_rate, levels), both, width, size_y)
     forward = [(i, i + 1) for i in range(size - 1)]
     backward = [(i + 1, i) for i in range(size - 1)]
     for block in range(BLOCKS):

time: 170 us -> 166 us (0.976)
  the two profiles are of different devices: /device:TPU:4 before, /device:TPU:2 now
where the time goes in v3:
time: 166 us; the launch traced here: 165 us
  starting transfers between devices  70.1 us (42%)
  blocking collectives  56.3 us (34%)
  Pallas kernels  30.5 us (18%)
  waiting for transfers between devices  5.16 us (3%)
  other arithmetic  1.88 us (1%)
    ppermute x8, starting transfers between devices, local(): lax.ppermute(p, 'prot', backward)  54.6 us
    all_to_all x1, blocking collectives, local(): both = lax.all_to_all(both, 'gene', 0, 0, tiled=True)  33.3 us
    pallas_call x8, Pallas kernels, run_block(): pl.pallas_call(partial(block_kernel, mode, block, chunk), out_shape=out,...  25.4 us
    all_to_all x1, blocking collectives, local(): done = lax.all_to_all(done, 'gene', 0, 0, tiled=True)  23 us
    ppermute x8, starting transfers between devices, local(): lax.ppermute(p, 'prot', forward)  15.5 us
    ppermute x8, waiting for transfers between devices, local(): lax.ppermute(p, 'prot', backward)  5.14 us
    pallas_call x2, Pallas kernels, enter(): pl.pallas_call(partial(entry_kernel, chunk, width * size_y), out_shape=ja...  4.34 us
  transfers between devices with their start and end apart: 16, of which 1 were waited for; matrix products, arithmetic and copies ran while one was open for 0% of the time, Pallas kernels for 14%

profile of v3, /device:TPU:2, one launch (start us, length us, event | category | flops | bytes accessed | tf_op | source)
XLA Modules:
  0.0 165.4 jit_solution(10674526726771386488)
XLA Ops:
  0.9 1.2 pad_maximum_fusion
  2.1 33.3 %all_to_all.10.both = f32[16,104,128]{2,1,0:T(8,128)S(1)} all-to-all(f32[16,104,128]{2,1,0:T(8,128)S(1)} %pad_maximum_fusion), channel_id=1, replica_groups=mesh['gene'=16,'prot'=32] {'gene'}, dimensions={0} | all-to-all | bytes 1703936 | tf_op jit(solution)/shard_map/all_to_all | solution.py:255
  35.4 2.2 %enter0.1.own = f32[6,16,8,128]{3,2,1,0:T(8,128)S(1)} custom-call(s32[4]{0:T(128)S(1)} %copy-done, f32[16,104,128]{2,1,0:T(8,128)S(1)} %all_to_all.10.both), custom_call_target="tpu_custom_call" | custom-call | tf_op jit(solution)/shard_map/enter0/pallas_call | solution.py:65
  37.6 2.1 %collective-permute-start.8 = (f32[6,16,8,128]{3,2,1,0:T(8,128)S(1)}, f32[6,16,8,128]{3,2,1,0:T(8,128)S(1)}, u32[]{:S(2)}, u32[]{:S(2)}) collective-permute-start(f32[6,16,8,128]{3,2,1,0:T(8,128)S(1)} %enter0.1.own), channel_id=1, source_target_pairs={{0,1},{1,2},{2,3},{3,4},{4,5},{5,6},{6,7},{7,8},{8,9},{9,10},{10,1... | collective-permute-start | bytes 1179656 | tf_op jit(solution)/shard_map/ppermute | solution.py:262
  39.7 7.9 %collective-permute-start.9 = (f32[6,16,8,128]{3,2,1,0:T(8,128)S(1)}, f32[6,16,8,128]{3,2,1,0:T(8,128)S(1)}, u32[]{:S(2)}, u32[]{:S(2)}) collective-permute-start(f32[6,16,8,128]{3,2,1,0:T(8,128)S(1)} %enter0.1.own), channel_id=1, source_target_pairs={{1,0},{2,1},{3,2},{4,3},{5,4},{6,5},{7,6},{8,7},{9,8},{10,9},{11,1... | collective-permute-start | bytes 1179656 | tf_op jit(solution)/shard_map/ppermute | solution.py:262
  47.6 2.2 %enter1.1.own = f32[6,16,8,128]{3,2,1,0:T(8,128)S(1)} custom-call(s32[4]{0:T(128)S(1)} %copy-done, f32[16,104,128]{2,1,0:T(8,128)S(1)} %all_to_all.10.both), custom_call_target="tpu_custom_call" | custom-call | tf_op jit(solution)/shard_map/enter1/pallas_call | solution.py:65
  49.8 1.9 %collective-permute-start = (f32[6,16,8,128]{3,2,1,0:T(8,128)S(1)}, f32[6,16,8,128]{3,2,1,0:T(8,128)S(1)}, u32[]{:S(2)}, u32[]{:S(2)}) collective-permute-start(f32[6,16,8,128]{3,2,1,0:T(8,128)S(1)} %enter1.1.own), channel_id=1, source_target_pairs={{0,1},{1,2},{2,3},{3,4},{4,5},{5,6},{6,7},{7,8},{8,9},{9,10},{10,1... | collective-permute-start | bytes 1179656 | tf_op jit(solution)/shard_map/ppermute | solution.py:262
  51.7 6.7 %collective-permute-start.1 = (f32[6,16,8,128]{3,2,1,0:T(8,128)S(1)}, f32[6,16,8,128]{3,2,1,0:T(8,128)S(1)}, u32[]{:S(2)}, u32[]{:S(2)}) collective-permute-start(f32[6,16,8,128]{3,2,1,0:T(8,128)S(1)} %enter1.1.own), channel_id=1, source_target_pairs={{1,0},{2,1},{3,2},{4,3},{5,4},{6,5},{7,6},{8,7},{9,8},{10,9},{11,1... | collective-permute-start | bytes 1179656 | tf_op jit(solution)/shard_map/ppermute | solution.py:262
  58.4 0.7 tables.1
  59.1 2.8 %block0_0.1.own = f32[6,16,8,128]{3,2,1,0:T(8,128)S(1)} custom-call(s32[4]{0:T(128)S(1)} %copy-done, f32[6,16,8,128]{3,2,1,0:T(8,128)S(1)} %enter0.1.own, f32[6,16,8,128]{3,2,1,0:T(8,128)S(1)} %collective-permute-done.8.left, f32[6,16,8,128]{3,2,1,0:T(8,128)S(1)} %collective-permute-done.9.right, f32[2,2,18,8,128]{4,3,2,1,0:T(8,128)S(1)} %get-tuple-element.13.x_table, ...), custom_call_target="tpu_custom_call" | custom-call | flops 15138816 | bytes 1572864 | tf_op jit(solution)/shard_map/block0_0/pallas_call | solution.py:237
  61.9 1.9 %collective-permute-start.10 = (f32[6,16,8,128]{3,2,1,0:T(8,128)S(1)}, f32[6,16,8,128]{3,2,1,0:T(8,128)S(1)}, u32[]{:S(2)}, u32[]{:S(2)}) collective-permute-start(f32[6,16,8,128]{3,2,1,0:T(8,128)S(1)} %block0_0.1.own), channel_id=1, source_target_pairs={{0,1},{1,2},{2,3},{3,4},{4,5},{5,6},{6,7},{7,8},{8,9},{9,10},{10,1... | collective-permute-start | bytes 1179656 | tf_op jit(solution)/shard_map/ppermute | solution.py:262
  63.8 6.7 %collective-permute-start.11 = (f32[6,16,8,128]{3,2,1,0:T(8,128)S(1)}, f32[6,16,8,128]{3,2,1,0:T(8,128)S(1)}, u32[]{:S(2)}, u32[]{:S(2)}) collective-permute-start(f32[6,16,8,128]{3,2,1,0:T(8,128)S(1)} %block0_0.1.own), channel_id=1, source_target_pairs={{1,0},{2,1},{3,2},{4,3},{5,4},{6,5},{7,6},{8,7},{9,8},{10,9},{11,1... | collective-permute-start | bytes 1179656 | tf_op jit(solution)/shard_map/ppermute | solution.py:262
  70.5 2.8 %block0_1.1.own = f32[6,16,8,128]{3,2,1,0:T(8,128)S(1)} custom-call(s32[4]{0:T(128)S(1)} %copy-done, f32[6,16,8,128]{3,2,1,0:T(8,128)S(1)} %enter1.1.own, f32[6,16,8,128]{3,2,1,0:T(8,128)S(1)} %collective-permute-done.left, f32[6,16,8,128]{3,2,1,0:T(8,128)S(1)} %collective-permute-done.1.right, f32[2,2,18,8,128]{4,3,2,1,0:T(8,128)S(1)} %get-tuple-element.13.x_table, ...), custom_call_target="tpu_custom_call" | custom-call | flops 15138816 | bytes 1572864 | tf_op jit(solution)/shard_map/block0_1/pallas_call | solution.py:237
  73.3 1.9 %collective-permute-start.2 = (f32[6,16,8,128]{3,2,1,0:T(8,128)S(1)}, f32[6,16,8,128]{3,2,1,0:T(8,128)S(1)}, u32[]{:S(2)}, u32[]{:S(2)}) collective-permute-start(f32[6,16,8,128]{3,2,1,0:T(8,128)S(1)} %block0_1.1.own), channel_id=1, source_target_pairs={{0,1},{1,2},{2,3},{3,4},{4,5},{5,6},{6,7},{7,8},{8,9},{9,10},{10,1... | collective-permute-start | bytes 1179656 | tf_op jit(solution)/shard_map/ppermute | solution.py:262
  75.2 6.7 %collective-permute-start.3 = (f32[6,16,8,128]{3,2,1,0:T(8,128)S(1)}, f32[6,16,8,128]{3,2,1,0:T(8,128)S(1)}, u32[]{:S(2)}, u32[]{:S(2)}) collective-permute-start(f32[6,16,8,128]{3,2,1,0:T(8,128)S(1)} %block0_1.1.own), channel_id=1, source_target_pairs={{1,0},{2,1},{3,2},{4,3},{5,4},{6,5},{7,6},{8,7},{9,8},{10,9},{11,1... | collective-permute-start | bytes 1179656 | tf_op jit(solution)/shard_map/ppermute | solution.py:262
  81.9 2.8 %block1_0.1.own = f32[6,16,8,128]{3,2,1,0:T(8,128)S(1)} custom-call(s32[4]{0:T(128)S(1)} %copy-done, f32[6,16,8,128]{3,2,1,0:T(8,128)S(1)} %block0_0.1.own, f32[6,16,8,128]{3,2,1,0:T(8,128)S(1)} %collective-permute-done.10.left, f32[6,16,8,128]{3,2,1,0:T(8,128)S(1)} %collective-permute-done.11.right, f32[2,2,18,8,128]{4,3,2,1,0:T(8,128)S(1)} %get-tuple-element.13.x_table, ...), custom_call_target="tpu_custom_call" | custom-call | flops 15138816 | bytes 1572864 | tf_op jit(solution)/shard_map/block1_0/pallas_call | solution.py:237
  84.7 1.9 %collective-permute-start.12 = (f32[6,16,8,128]{3,2,1,0:T(8,128)S(1)}, f32[6,16,8,128]{3,2,1,0:T(8,128)S(1)}, u32[]{:S(2)}, u32[]{:S(2)}) collective-permute-start(f32[6,16,8,128]{3,2,1,0:T(8,128)S(1)} %block1_0.1.own), channel_id=1, source_target_pairs={{0,1},{1,2},{2,3},{3,4},{4,5},{5,6},{6,7},{7,8},{8,9},{9,10},{10,1... | collective-permute-start | bytes 1179656 | tf_op jit(solution)/shard_map/ppermute | solution.py:262
  86.6 6.7 %collective-permute-start.13 = (f32[6,16,8,128]{3,2,1,0:T(8,128)S(1)}, f32[6,16,8,128]{3,2,1,0:T(8,128)S(1)}, u32[]{:S(2)}, u32[]{:S(2)}) collective-permute-start(f32[6,16,8,128]{3,2,1,0:T(8,128)S(1)} %block1_0.1.own), channel_id=1, source_target_pairs={{1,0},{2,1},{3,2},{4,3},{5,4},{6,5},{7,6},{8,7},{9,8},{10,9},{11,1... | collective-permute-start | bytes 1179656 | tf_op jit(solution)/shard_map/ppermute | solution.py:262
  93.3 2.8 %block1_1.1.own = f32[6,16,8,128]{3,2,1,0:T(8,128)S(1)} custom-call(s32[4]{0:T(128)S(1)} %copy-done, f32[6,16,8,128]{3,2,1,0:T(8,128)S(1)} %block0_1.1.own, f32[6,16,8,128]{3,2,1,0:T(8,128)S(1)} %collective-permute-done.2.left, f32[6,16,8,128]{3,2,1,0:T(8,128)S(1)} %collective-permute-done.3.right, f32[2,2,18,8,128]{4,3,2,1,0:T(8,128)S(1)} %get-tuple-element.13.x_table, ...), custom_call_target="tpu_custom_call" | custom-call | flops 15138816 | bytes 1572864 | tf_op jit(solution)/shard_map/block1_1/pallas_call | solution.py:237
  96.1 1.9 %collective-permute-start.4 = (f32[6,16,8,128]{3,2,1,0:T(8,128)S(1)}, f32[6,16,8,128]{3,2,1,0:T(8,128)S(1)}, u32[]{:S(2)}, u32[]{:S(2)}) collective-permute-start(f32[6,16,8,128]{3,2,1,0:T(8,128)S(1)} %block1_1.1.own), channel_id=1, source_target_pairs={{0,1},{1,2},{2,3},{3,4},{4,5},{5,6},{6,7},{7,8},{8,9},{9,10},{10,1... | collective-permute-start | bytes 1179656 | tf_op jit(solution)/shard_map/ppermute | solution.py:262
  98.0 6.8 %collective-permute-start.5 = (f32[6,16,8,128]{3,2,1,0:T(8,128)S(1)}, f32[6,16,8,128]{3,2,1,0:T(8,128)S(1)}, u32[]{:S(2)}, u32[]{:S(2)}) collective-permute-start(f32[6,16,8,128]{3,2,1,0:T(8,128)S(1)} %block1_1.1.own), channel_id=1, source_target_pairs={{1,0},{2,1},{3,2},{4,3},{5,4},{6,5},{7,6},{8,7},{9,8},{10,9},{11,1... | collective-permute-start | bytes 1179656 | tf_op jit(solution)/shard_map/ppermute | solution.py:262
  104.9 2.8 %block2_0.1.own = f32[6,16,8,128]{3,2,1,0:T(8,128)S(1)} custom-call(s32[4]{0:T(128)S(1)} %copy-done, f32[6,16,8,128]{3,2,1,0:T(8,128)S(1)} %block1_0.1.own, f32[6,16,8,128]{3,2,1,0:T(8,128)S(1)} %collective-permute-done.12.left, f32[6,16,8,128]{3,2,1,0:T(8,128)S(1)} %collective-permute-done.13.right, f32[2,2,18,8,128]{4,3,2,1,0:T(8,128)S(1)} %get-tuple-element.13.x_table, ...), custom_call_target="tpu_custom_call" | custom-call | flops 15138816 | bytes 1572864 | tf_op jit(solution)/shard_map/block2_0/pallas_call | solution.py:237
  107.7 1.9 %collective-permute-start.14 = (f32[6,16,8,128]{3,2,1,0:T(8,128)S(1)}, f32[6,16,8,128]{3,2,1,0:T(8,128)S(1)}, u32[]{:S(2)}, u32[]{:S(2)}) collective-permute-start(f32[6,16,8,128]{3,2,1,0:T(8,128)S(1)} %block2_0.1.own), channel_id=1, source_target_pairs={{0,1},{1,2},{2,3},{3,4},{4,5},{5,6},{6,7},{7,8},{8,9},{9,10},{10,1... | collective-permute-start | bytes 1179656 | tf_op jit(solution)/shard_map/ppermute | solution.py:262
  109.6 6.7 %collective-permute-start.15 = (f32[6,16,8,128]{3,2,1,0:T(8,128)S(1)}, f32[6,16,8,128]{3,2,1,0:T(8,128)S(1)}, u32[]{:S(2)}, u32[]{:S(2)}) collective-permute-start(f32[6,16,8,128]{3,2,1,0:T(8,128)S(1)} %block2_0.1.own), channel_id=1, source_target_pairs={{1,0},{2,1},{3,2},{4,3},{5,4},{6,5},{7,6},{8,7},{9,8},{10,9},{11,1... | collective-permute-start | bytes 1179656 | tf_op jit(solution)/shard_map/ppermute | solution.py:262
  116.3 2.8 %block2_1.1.own = f32[6,16,8,128]{3,2,1,0:T(8,128)S(1)} custom-call(s32[4]{0:T(128)S(1)} %copy-done, f32[6,16,8,128]{3,2,1,0:T(8,128)S(1)} %block1_1.1.own, f32[6,16,8,128]{3,2,1,0:T(8,128)S(1)} %collective-permute-done.4.left, f32[6,16,8,128]{3,2,1,0:T(8,128)S(1)} %collective-permute-done.5.right, f32[2,2,18,8,128]{4,3,2,1,0:T(8,128)S(1)} %get-tuple-element.13.x_table, ...), custom_call_target="tpu_custom_call" | custom-call | flops 15138816 | bytes 1572864 | tf_op jit(solution)/shard_map/block2_1/pallas_call | solution.py:237
  119.1 1.9 %collective-permute-start.6 = (f32[6,16,8,128]{3,2,1,0:T(8,128)S(1)}, f32[6,16,8,128]{3,2,1,0:T(8,128)S(1)}, u32[]{:S(2)}, u32[]{:S(2)}) collective-permute-start(f32[6,16,8,128]{3,2,1,0:T(8,128)S(1)} %block2_1.1.own), channel_id=1, source_target_pairs={{0,1},{1,2},{2,3},{3,4},{4,5},{5,6},{6,7},{7,8},{8,9},{9,10},{10,1... | collective-permute-start | bytes 1179656 | tf_op jit(solution)/shard_map/ppermute | solution.py:262
  121.0 6.7 %collective-permute-start.7 = (f32[6,16,8,128]{3,2,1,0:T(8,128)S(1)}, f32[6,16,8,128]{3,2,1,0:T(8,128)S(1)}, u32[]{:S(2)}, u32[]{:S(2)}) collective-permute-start(f32[6,16,8,128]{3,2,1,0:T(8,128)S(1)} %block2_1.1.own), channel_id=1, source_target_pairs={{1,0},{2,1},{3,2},{4,3},{5,4},{6,5},{7,6},{8,7},{9,8},{10,9},{11,1... | collective-permute-start | bytes 1179656 | tf_op jit(solution)/shard_map/ppermute | solution.py:262
  127.7 4.3 %block3_0.1.rest_0_ = f32[768,128]{1,0:T(8,128)S(1)} custom-call(s32[4]{0:T(128)S(1)} %copy-done, f32[6,16,8,128]{3,2,1,0:T(8,128)S(1)} %block2_0.1.own, f32[6,16,8,128]{3,2,1,0:T(8,128)S(1)} %collective-permute-done.14.left, f32[6,16,8,128]{3,2,1,0:T(8,128)S(1)} %collective-permute-done.15.right, f32[2,2,18,8,128]{4,3,2,1,0:T(8,128)S(1)} %get-tuple-element.13.x_table, ...), custom_call_target="tpu_custom_call" | custom-call | flops 15138816 | bytes 1572864 | tf_op jit(solution)/shard_map/block3_0/pallas_call | solution.py:237
  132.0 5.1 %collective-permute-done.7.right = f32[6,16,8,128]{3,2,1,0:T(8,128)S(1)} collective-permute-done((f32[6,16,8,128]{3,2,1,0:T(8,128)S(1)}, f32[6,16,8,128]{3,2,1,0:T(8,128)S(1)}, u32[]{:S(2)}, u32[]{:S(2)}) %collective-permute-start.7) | collective-permute-done | bytes 393248 | tf_op jit(solution)/shard_map/ppermute | solution.py:262
  137.1 4.4 %block3_1.1 = f32[16,96,128]{2,1,0:T(8,128)S(1)} custom-call(s32[4]{0:T(128)S(1)} %copy-done, f32[6,16,8,128]{3,2,1,0:T(8,128)S(1)} %block2_1.1.own, f32[6,16,8,128]{3,2,1,0:T(8,128)S(1)} %collective-permute-done.6.left, f32[6,16,8,128]{3,2,1,0:T(8,128)S(1)} %collective-permute-done.7.right, f32[2,2,18,8,128]{4,3,2,1,0:T(8,128)S(1)} %get-tuple-element.13.x_table, ...), custom_call_target="tpu_custom_call" | custom-call | flops 15138816 | bytes 1572864 | tf_op jit(solution)/shard_map/block3_1/pallas_call | solution.py:237
  141.5 23.0 %all_to_all.11 = f32[16,96,128]{2,1,0:T(8,128)S(1)} all-to-all(f32[16,96,128]{2,1,0:T(8,128)S(1)} %block3_1.1), channel_id=1, replica_groups=mesh['gene'=16,'prot'=32] {'gene'}, dimensions={0} | all-to-all | bytes 1572864 | tf_op jit(solution)/shard_map/all_to_all | solution.py:268
  164.5 0.9 copy.10
  (27 shorter events, 0.9 us)
Async XLA Ops:
  2.1 33.3 %copy-start = (s32[4]{0:T(128)S(1)}, s32[4]{0:T(128)}, u32[]{:S(2)}) copy-start(s32[4]{0:T(128)} %order.21) | copy-start | bytes 52
  37.6 20.8 %copy-start.1 = (f32[8]{0:T(128)S(1)}, f32[8]{0:T(128)}, u32[]{:S(2)}) copy-start(f32[8]{0:T(128)} %on_rate.1) | copy-start | bytes 100
  37.6 20.8 %copy-start.2 = (f32[8]{0:T(128)S(1)}, f32[8]{0:T(128)}, u32[]{:S(2)}) copy-start(f32[8]{0:T(128)} %off_rate.1) | copy-start | bytes 100
  37.6 20.8 %copy-start.3 = (f32[8]{0:T(128)S(1)}, f32[8]{0:T(128)}, u32[]{:S(2)}) copy-start(f32[8]{0:T(128)} %levels) | copy-start | bytes 100
  37.6 21.5 %collective-permute-start.8 = (f32[6,16,8,128]{3,2,1,0:T(8,128)S(1)}, f32[6,16,8,128]{3,2,1,0:T(8,128)S(1)}, u32[]{:S(2)}, u32[]{:S(2)}) collective-permute-start(f32[6,16,8,128]{3,2,1,0:T(8,128)S(1)} %enter0.1.own), channel_id=1, source_target_pairs={{0,1},{1,2},{2,3},{3,4},{4,5},{5,6},{6,7},{7,8},{8,9},{9,10},{10,1... | collective-permute-start | bytes 1179656 | tf_op jit(solution)/shard_map/ppermute | solution.py:262
  39.7 19.4 %collective-permute-start.9 = (f32[6,16,8,128]{3,2,1,0:T(8,128)S(1)}, f32[6,16,8,128]{3,2,1,0:T(8,128)S(1)}, u32[]{:S(2)}, u32[]{:S(2)}) collective-permute-start(f32[6,16,8,128]{3,2,1,0:T(8,128)S(1)} %enter0.1.own), channel_id=1, source_target_pairs={{1,0},{2,1},{3,2},{4,3},{5,4},{6,5},{7,6},{8,7},{9,8},{10,9},{11,1... | collective-permute-start | bytes 1179656 | tf_op jit(solution)/shard_map/ppermute | solution.py:262
  49.8 20.7 %collective-permute-start = (f32[6,16,8,128]{3,2,1,0:T(8,128)S(1)}, f32[6,16,8,128]{3,2,1,0:T(8,128)S(1)}, u32[]{:S(2)}, u32[]{:S(2)}) collective-permute-start(f32[6,16,8,128]{3,2,1,0:T(8,128)S(1)} %enter1.1.own), channel_id=1, source_target_pairs={{0,1},{1,2},{2,3},{3,4},{4,5},{5,6},{6,7},{7,8},{8,9},{9,10},{10,1... | collective-permute-start | bytes 1179656 | tf_op jit(solution)/shard_map/ppermute | solution.py:262
  51.7 18.8 %collective-permute-start.1 = (f32[6,16,8,128]{3,2,1,0:T(8,128)S(1)}, f32[6,16,8,128]{3,2,1,0:T(8,128)S(1)}, u32[]{:S(2)}, u32[]{:S(2)}) collective-permute-start(f32[6,16,8,128]{3,2,1,0:T(8,128)S(1)} %enter1.1.own), channel_id=1, source_target_pairs={{1,0},{2,1},{3,2},{4,3},{5,4},{6,5},{7,6},{8,7},{9,8},{10,9},{11,1... | collective-permute-start | bytes 1179656 | tf_op jit(solution)/shard_map/ppermute | solution.py:262
  61.9 20.0 %collective-permute-start.10 = (f32[6,16,8,128]{3,2,1,0:T(8,128)S(1)}, f32[6,16,8,128]{3,2,1,0:T(8,128)S(1)}, u32[]{:S(2)}, u32[]{:S(2)}) collective-permute-start(f32[6,16,8,128]{3,2,1,0:T(8,128)S(1)} %block0_0.1.own), channel_id=1, source_target_pairs={{0,1},{1,2},{2,3},{3,4},{4,5},{5,6},{6,7},{7,8},{8,9},{9,10},{10,1... | collective-permute-start | bytes 1179656 | tf_op jit(solution)/shard_map/ppermute | solution.py:262
  63.8 18.1 %collective-permute-start.11 = (f32[6,16,8,128]{3,2,1,0:T(8,128)S(1)}, f32[6,16,8,128]{3,2,1,0:T(8,128)S(1)}, u32[]{:S(2)}, u32[]{:S(2)}) collective-permute-start(f32[6,16,8,128]{3,2,1,0:T(8,128)S(1)} %block0_0.1.own), channel_id=1, source_target_pairs={{1,0},{2,1},{3,2},{4,3},{5,4},{6,5},{7,6},{8,7},{9,8},{10,9},{11,1... | collective-permute-start | bytes 1179656 | tf_op jit(solution)/shard_map/ppermute | solution.py:262
  73.3 20.0 %collective-permute-start.2 = (f32[6,16,8,128]{3,2,1,0:T(8,128)S(1)}, f32[6,16,8,128]{3,2,1,0:T(8,128)S(1)}, u32[]{:S(2)}, u32[]{:S(2)}) collective-permute-start(f32[6,16,8,128]{3,2,1,0:T(8,128)S(1)} %block0_1.1.own), channel_id=1, source_target_pairs={{0,1},{1,2},{2,3},{3,4},{4,5},{5,6},{6,7},{7,8},{8,9},{9,10},{10,1... | collective-permute-start | bytes 1179656 | tf_op jit(solution)/shard_map/ppermute | solution.py:262
  75.2 18.1 %collective-permute-start.3 = (f32[6,16,8,128]{3,2,1,0:T(8,128)S(1)}, f32[6,16,8,128]{3,2,1,0:T(8,128)S(1)}, u32[]{:S(2)}, u32[]{:S(2)}) collective-permute-start(f32[6,16,8,128]{3,2,1,0:T(8,128)S(1)} %block0_1.1.own), channel_id=1, source_target_pairs={{1,0},{2,1},{3,2},{4,3},{5,4},{6,5},{7,6},{8,7},{9,8},{10,9},{11,1... | collective-permute-start | bytes 1179656 | tf_op jit(solution)/shard_map/ppermute | solution.py:262
  84.7 20.2 %collective-permute-start.12 = (f32[6,16,8,128]{3,2,1,0:T(8,128)S(1)}, f32[6,16,8,128]{3,2,1,0:T(8,128)S(1)}, u32[]{:S(2)}, u32[]{:S(2)}) collective-permute-start(f32[6,16,8,128]{3,2,1,0:T(8,128)S(1)} %block1_0.1.own), channel_id=1, source_target_pairs={{0,1},{1,2},{2,3},{3,4},{4,5},{5,6},{6,7},{7,8},{8,9},{9,10},{10,1... | collective-permute-start | bytes 1179656 | tf_op jit(solution)/shard_map/ppermute | solution.py:262
  86.6 18.3 %collective-permute-start.13 = (f32[6,16,8,128]{3,2,1,0:T(8,128)S(1)}, f32[6,16,8,128]{3,2,1,0:T(8,128)S(1)}, u32[]{:S(2)}, u32[]{:S(2)}) collective-permute-start(f32[6,16,8,128]{3,2,1,0:T(8,128)S(1)} %block1_0.1.own), channel_id=1, source_target_pairs={{1,0},{2,1},{3,2},{4,3},{5,4},{6,5},{7,6},{8,7},{9,8},{10,9},{11,1... | collective-permute-start | bytes 1179656 | tf_op jit(solution)/shard_map/ppermute | solution.py:262
  96.1 20.2 %collective-permute-start.4 = (f32[6,16,8,128]{3,2,1,0:T(8,128)S(1)}, f32[6,16,8,128]{3,2,1,0:T(8,128)S(1)}, u32[]{:S(2)}, u32[]{:S(2)}) collective-permute-start(f32[6,16,8,128]{3,2,1,0:T(8,128)S(1)} %block1_1.1.own), channel_id=1, source_target_pairs={{0,1},{1,2},{2,3},{3,4},{4,5},{5,6},{6,7},{7,8},{8,9},{9,10},{10,1... | collective-permute-start | bytes 1179656 | tf_op jit(solution)/shard_map/ppermute | solution.py:262
  98.0 18.3 %collective-permute-start.5 = (f32[6,16,8,128]{3,2,1,0:T(8,128)S(1)}, f32[6,16,8,128]{3,2,1,0:T(8,128)S(1)}, u32[]{:S(2)}, u32[]{:S(2)}) collective-permute-start(f32[6,16,8,128]{3,2,1,0:T(8,128)S(1)} %block1_1.1.own), channel_id=1, source_target_pairs={{1,0},{2,1},{3,2},{4,3},{5,4},{6,5},{7,6},{8,7},{9,8},{10,9},{11,1... | collective-permute-start | bytes 1179656 | tf_op jit(solution)/shard_map/ppermute | solution.py:262
  107.7 20.0 %collective-permute-start.14 = (f32[6,16,8,128]{3,2,1,0:T(8,128)S(1)}, f32[6,16,8,128]{3,2,1,0:T(8,128)S(1)}, u32[]{:S(2)}, u32[]{:S(2)}) collective-permute-start(f32[6,16,8,128]{3,2,1,0:T(8,128)S(1)} %block2_0.1.own), channel_id=1, source_target_pairs={{0,1},{1,2},{2,3},{3,4},{4,5},{5,6},{6,7},{7,8},{8,9},{9,10},{10,1... | collective-permute-start | bytes 1179656 | tf_op jit(solution)/shard_map/ppermute | solution.py:262
  109.6 18.1 %collective-permute-start.15 = (f32[6,16,8,128]{3,2,1,0:T(8,128)S(1)}, f32[6,16,8,128]{3,2,1,0:T(8,128)S(1)}, u32[]{:S(2)}, u32[]{:S(2)}) collective-permute-start(f32[6,16,8,128]{3,2,1,0:T(8,128)S(1)} %block2_0.1.own), channel_id=1, source_target_pairs={{1,0},{2,1},{3,2},{4,3},{5,4},{6,5},{7,6},{8,7},{9,8},{10,9},{11,1... | collective-permute-start | bytes 1179656 | tf_op jit(solution)/shard_map/ppermute | solution.py:262
  119.1 12.9 %collective-permute-start.6 = (f32[6,16,8,128]{3,2,1,0:T(8,128)S(1)}, f32[6,16,8,128]{3,2,1,0:T(8,128)S(1)}, u32[]{:S(2)}, u32[]{:S(2)}) collective-permute-start(f32[6,16,8,128]{3,2,1,0:T(8,128)S(1)} %block2_1.1.own), channel_id=1, source_target_pairs={{0,1},{1,2},{2,3},{3,4},{4,5},{5,6},{6,7},{7,8},{8,9},{9,10},{10,1... | collective-permute-start | bytes 1179656 | tf_op jit(solution)/shard_map/ppermute | solution.py:262
  121.0 16.1 %collective-permute-start.7 = (f32[6,16,8,128]{3,2,1,0:T(8,128)S(1)}, f32[6,16,8,128]{3,2,1,0:T(8,128)S(1)}, u32[]{:S(2)}, u32[]{:S(2)}) collective-permute-start(f32[6,16,8,128]{3,2,1,0:T(8,128)S(1)} %block2_1.1.own), channel_id=1, source_target_pairs={{1,0},{2,1},{3,2},{4,3},{5,4},{6,5},{7,6},{8,7},{9,8},{10,9},{11,1... | collective-permute-start | bytes 1179656 | tf_op jit(solution)/shard_map/ppermute | solution.py:262
